TPU v7x, 128 devices: a whole 4x4x4 slice. The times are simulated.
128 devices in a mesh: lat: 4 (over y), lon: 32 (over z, x, core).
Axes of the slice: x: 4, y: 4, z: 4, core: 2. Of those that a mesh axis runs over, the one named last changes fastest.
Arguments:
- grid_x: bfloat16 [32768, 227], P(('lat', 'lon')), may hold values from -6 to 6
- mesh_in: bfloat16 [32768, 512], P(('lat', 'lon')), may hold values from -6 to 6
- mesh_grad: bfloat16 [32768, 512], P(('lat', 'lon')), may hold values from -6 to 6
- embed_in: bfloat16 [227, 512], replicated, may hold values from -0.375 to 0.375
- enc_weights: bfloat16 [7, 512, 512], replicated, may hold values from -0.25 to 0.25
- proc_weights: bfloat16 [2, 6, 512, 512], replicated, may hold values from -0.25 to 0.25
- g2m_grid: int32 [5120], P(('lat', 'lon')), may hold values from 0 to 7
- g2m_mesh: int32 [5120], P(('lat', 'lon')), may hold values from 0 to 1023, as said below
- mesh_send: int32 [2048], P(('lat', 'lon')), may hold values from 0 to 11, as said below
- mesh_recv: int32 [2048], P(('lat', 'lon')), may hold values from 0 to 7
- halo_idx: int32 [128, 4, 1], P(('lat', 'lon')), may hold values from 0 to 7
Outputs:
- mesh_out: bfloat16 [32768, 512], P(('lat', 'lon'))
- mesh_in_grad: float32 [32768, 512], P(('lat', 'lon'))
- enc_grads: float32 [7, 512, 512], P(None, ('lat', 'lon'))
- proc_grads: float32 [2, 6, 512, 512], P(None, None, ('lat', 'lon'))
- embed_grad: float32 [227, 512], P(None, ('lat', 'lon'))
Inputs may be any that keep to these rules, and one draw needn't show every extreme that they name: `g2m_mesh`: the mesh block of an edge block lies on a device with the same lat index as the edge block's device. Among one device's 40 edge blocks at most 2 name mesh blocks of any one device; in every lat row one device receives exactly 2 from every device of the row. `mesh_send`: slots below 8 are local blocks; then 1 slots each for the blocks shown by the lower-lat, upper-lat, lower-lon and upper-lon neighbour. Devices of the first lat index name no lower-lat slot, of the last none upper-lat; every other neighbour slot is named by some edge block of the device. halo_idx[d, k] lists blocks of device d shown to its neighbour k: 0 lower lat, 1 upper lat, 2 lower lon, 3 upper lon.
All inputs are finite; a program needn't handle non-finite values.
Results may differ from a plain program's by a relative error of at most 0.03.
Values may be sent and summed in bfloat16 or wider, within the bound.
A program may use at most 192 MiB of HBM per device.

v0:
```python
import jax
import jax.numpy as jnp
from jax import lax
from jax.sharding import PartitionSpec as P

B = 32
ROUNDS = 2


EPSILON = 1e-05
HIGHEST_PRECISION = lax.Precision.HIGHEST


def extended(value, sides, width, wrap):
    for axis, dim in sides:
        peers, length = (lax.axis_size(axis), value.shape[dim])
        up = [(i, (i + 1) % peers) for i in range(peers if wrap else peers - 1)]
        down = [(j, i) for i, j in up]
        last = lax.slice_in_dim(value, length - width, length, axis=dim)
        leading = lax.slice_in_dim(value, 0, width, axis=dim)
        before = lax.ppermute(last, axis, up)
        after = lax.ppermute(leading, axis, down)
        value = jnp.concatenate([before, value, after], axis=dim)
    return value


def matmul(first_op, second_op):
    return jnp.dot(first_op, second_op, preferred_element_type=jnp.float32)


def outer_sum(first_op, second_op):
    return lax.dot_general(
        first_op, second_op, (((0,), (0,)), ((), ())), preferred_element_type=jnp.float32
    )


def by_transpose(grad_in, weight):
    return lax.dot_general(
        grad_in, weight, (((1,), (1,)), ((), ())), preferred_element_type=jnp.float32
    )


def norm_rows(values):
    average = jnp.mean(values, axis=-1, keepdims=True)
    centred = values - average
    inv_std = lax.rsqrt(jnp.mean(centred * centred, axis=-1, keepdims=True) + EPSILON)
    return (centred * inv_std, inv_std)


def norm_back(grad_in, normed, inv_std):
    return inv_std * (
        grad_in
        - jnp.mean(grad_in, axis=-1, keepdims=True)
        - normed * jnp.mean(grad_in * normed, axis=-1, keepdims=True)
    )


def swish_grad(values):
    sigmoid_v = jax.nn.sigmoid(values)
    return sigmoid_v * (1.0 + values * (1.0 - sigmoid_v))


def mesh_update(latent, summed, w_latent, w_summed, w_output):
    summed_bf = summed.astype(jnp.bfloat16)
    gate_in = matmul(latent, w_latent) + matmul(summed_bf, w_summed)
    hidden = jax.nn.silu(gate_in).astype(jnp.bfloat16)
    normed, inv_std = norm_rows(matmul(hidden, w_output))
    updated = (latent.astype(jnp.float32) + normed).astype(jnp.bfloat16)
    return (updated, (latent, summed_bf, gate_in, hidden, normed, inv_std))


def update_back(grad_new, cache, w_latent, w_summed, w_output):
    latent, summed_bf, gate_in, hidden, normed, inv_std = cache
    grad_out = norm_back(grad_new, normed, inv_std).astype(jnp.bfloat16)
    grad_hidden = by_transpose(grad_out, w_output)
    grad_wo = outer_sum(hidden, grad_out)
    grad_gate = (grad_hidden * swish_grad(gate_in)).astype(jnp.bfloat16)
    grad_latent = grad_new + by_transpose(grad_gate, w_latent)
    grad_summed = by_transpose(grad_gate, w_summed)
    return (
        grad_latent,
        grad_summed,
        outer_sum(latent, grad_gate),
        outer_sum(summed_bf, grad_gate),
        grad_wo,
    )


def on_device(
    grid_x,
    mesh_in,
    mesh_grad,
    embed_in,
    enc_weights,
    proc_weights,
    g2m_grid,
    g2m_mesh,
    mesh_send,
    mesh_recv,
    halo_idx,
):
    width = mesh_in.shape[1]
    lon_count = lax.axis_size("lon")
    edge_count = g2m_grid.shape[0]
    capacity = (edge_count + lon_count - 1) // lon_count
    slot_count = lon_count * capacity
    mesh_blocks = mesh_in.shape[0] // B
    grid_blocks = grid_x.shape[0] // B
    halo_blocks = halo_idx.shape[2]
    emb_pre = matmul(grid_x, embed_in)
    emb_act = jax.nn.silu(emb_pre).astype(jnp.bfloat16)
    grid_norm, grid_rstd = norm_rows(matmul(emb_act, enc_weights[0]))
    grid_lat = grid_norm.astype(jnp.bfloat16).reshape(grid_blocks, B, width)
    owners = g2m_mesh // mesh_blocks % lon_count
    owner_hot = (owners[:, None] == jnp.arange(lon_count, dtype=jnp.int32)[None, :]).astype(
        jnp.int32
    )
    ranks = jnp.sum(jnp.cumsum(owner_hot, axis=0) * owner_hot, axis=1) - 1
    slot_of = owners * capacity + ranks
    slot_hot = slot_of[None, :] == jnp.arange(slot_count, dtype=jnp.int32)[:, None]
    slot_used = jnp.any(slot_hot, axis=1)
    slot_edge = jnp.sum(
        jnp.where(slot_hot, jnp.arange(edge_count, dtype=jnp.int32)[None, :], 0), axis=1
    )
    send_blocks = jnp.where(
        slot_used[:, None, None], grid_lat[g2m_grid[slot_edge]], jnp.zeros((), jnp.bfloat16)
    )
    send_blocks = send_blocks.reshape(lon_count, capacity, B, width)
    send_dest = jnp.where(slot_used, g2m_mesh[slot_edge] % mesh_blocks, -1).reshape(
        lon_count, capacity
    )
    recv_proj = matmul(mesh_in, enc_weights[2]).reshape(mesh_blocks, B, width)
    blocks = lax.all_to_all(send_blocks, "lon", split_axis=0, concat_axis=0, tiled=True)
    dest_ids = lax.all_to_all(send_dest, "lon", split_axis=0, concat_axis=0, tiled=True)
    block_shape = blocks.shape
    is_valid = dest_ids >= 0
    picked = jnp.where(is_valid[..., None, None], recv_proj[jnp.maximum(dest_ids, 0)], 0.0)
    owner_edge_pre = matmul(blocks.reshape(-1, width), enc_weights[1]).reshape(block_shape) + picked
    owner_edge_act = jax.nn.silu(owner_edge_pre).astype(jnp.bfloat16)
    owner_message, owner_edge_rstd = norm_rows(
        matmul(owner_edge_act.reshape(-1, width), enc_weights[3])
    )
    g2m_msg = owner_message.reshape(block_shape)
    g2m_rstd = owner_edge_rstd.reshape(block_shape[:-1] + (1,))
    dest_hot = (dest_ids[..., None] == jnp.arange(mesh_blocks, dtype=jnp.int32)).astype(jnp.float32)
    g2m_sum = jnp.einsum("scm,scbl->mbl", dest_hot, g2m_msg, precision=HIGHEST_PRECISION).reshape(
        -1, width
    )
    latent, enc_cache = mesh_update(
        mesh_in, g2m_sum, enc_weights[4], enc_weights[5], enc_weights[6]
    )
    table_size = mesh_blocks + 4 * halo_blocks
    send_hot = (mesh_send[:, None] == jnp.arange(table_size, dtype=jnp.int32)).astype(jnp.float32)
    recv_hot = (mesh_recv[:, None] == jnp.arange(mesh_blocks, dtype=jnp.int32)).astype(jnp.float32)
    halo_flat = halo_idx[0].reshape(-1)
    return_hot = (halo_flat[:, None] == jnp.arange(mesh_blocks, dtype=jnp.int32)).astype(
        jnp.float32
    )
    caches = []
    for round_index in range(ROUNDS):
        weights = proc_weights[round_index]
        blocks_now = latent.reshape(mesh_blocks, B, width)
        local_proj = matmul(latent, weights[0]).reshape(mesh_blocks, B, width)
        lat_rim = extended(
            jnp.stack([blocks_now[halo_idx[0, 0]], blocks_now[halo_idx[0, 1]]]),
            (("lat", 0),),
            1,
            False,
        )
        lon_rim = extended(
            jnp.stack([blocks_now[halo_idx[0, 2]], blocks_now[halo_idx[0, 3]]]),
            (("lon", 0),),
            1,
            True,
        )
        halo_lat = jnp.concatenate([lat_rim[0], lat_rim[3], lon_rim[0], lon_rim[3]])
        halo_proj = matmul(halo_lat.reshape(-1, width), weights[0]).reshape(-1, B, width)
        ext_proj = jnp.concatenate([local_proj, halo_proj])
        recv_side = matmul(latent, weights[1]).reshape(mesh_blocks, B, width)
        edge_pre = (ext_proj[mesh_send] + recv_side[mesh_recv]).reshape(-1, width)
        edge_act = jax.nn.silu(edge_pre).astype(jnp.bfloat16)
        message, edge_rstd = norm_rows(matmul(edge_act, weights[2]))
        summed = jnp.einsum(
            "em,ebl->mbl", recv_hot, message.reshape(-1, B, width), precision=HIGHEST_PRECISION
        ).reshape(-1, width)
        new_latent, upd_cache = mesh_update(latent, summed, weights[3], weights[4], weights[5])
        caches.append((latent, edge_pre, edge_act, message, edge_rstd, upd_cache))
        latent = new_latent
    grad_h = mesh_grad.astype(jnp.float32)
    round_shards = [None] * ROUNDS
    for round_index in reversed(range(ROUNDS)):
        weights = proc_weights[round_index]
        before, edge_pre, edge_act, message, edge_rstd, upd_cache = caches[round_index]
        grad_h, grad_sum, grad_wh, grad_wa, grad_wo = update_back(
            grad_h, upd_cache, weights[3], weights[4], weights[5]
        )
        grad_msg = grad_sum.reshape(mesh_blocks, B, width)[mesh_recv].reshape(-1, width)
        grad_z = norm_back(grad_msg, message, edge_rstd).astype(jnp.bfloat16)
        grad_act = by_transpose(grad_z, weights[2])
        grad_we = outer_sum(edge_act, grad_z)
        grad_pre = (grad_act * swish_grad(edge_pre)).reshape(-1, B, width)
        grad_ext = jnp.einsum("es,ebl->sbl", send_hot, grad_pre, precision=HIGHEST_PRECISION)
        grad_recv = jnp.einsum("em,ebl->mbl", recv_hot, grad_pre, precision=HIGHEST_PRECISION)
        rims = grad_ext[mesh_blocks:].reshape(4, halo_blocks, B, width)
        back_lat = extended(rims[0:2].astype(jnp.bfloat16), (("lat", 0),), 1, False).astype(
            jnp.float32
        )
        back_lon = extended(rims[2:4].astype(jnp.bfloat16), (("lon", 0),), 1, True).astype(
            jnp.float32
        )
        returned = jnp.concatenate([back_lat[0], back_lat[3], back_lon[0], back_lon[3]])
        grad_proj = grad_ext[:mesh_blocks] + jnp.einsum(
            "km,kbl->mbl", return_hot, returned, precision=HIGHEST_PRECISION
        )
        grad_proj_bf = grad_proj.reshape(-1, width).astype(jnp.bfloat16)
        grad_recv_bf = grad_recv.reshape(-1, width).astype(jnp.bfloat16)
        grad_h = (
            grad_h + by_transpose(grad_proj_bf, weights[0]) + by_transpose(grad_recv_bf, weights[1])
        )
        grad_terms = jnp.stack(
            [
                outer_sum(before, grad_proj_bf),
                outer_sum(before, grad_recv_bf),
                grad_we,
                grad_wh,
                grad_wa,
                grad_wo,
            ]
        )
        round_shards[round_index] = lax.psum_scatter(
            grad_terms, ("lat", "lon"), scatter_dimension=1, tiled=True
        )
    grad_h, grad_sum, grad_nh, grad_na, grad_n2 = update_back(
        grad_h, enc_cache, enc_weights[4], enc_weights[5], enc_weights[6]
    )
    is_valid = dest_ids >= 0
    grad_msg = jnp.where(
        is_valid[..., None, None],
        grad_sum.reshape(mesh_blocks, B, width)[jnp.maximum(dest_ids, 0)],
        0.0,
    ).reshape(-1, width)
    grad_z = norm_back(grad_msg, g2m_msg.reshape(-1, width), g2m_rstd.reshape(-1, 1)).astype(
        jnp.bfloat16
    )
    grad_act = by_transpose(grad_z, enc_weights[3])
    grad_a2 = outer_sum(owner_edge_act.reshape(-1, width), grad_z)
    grad_pre = grad_act * swish_grad(owner_edge_pre.reshape(-1, width))
    grad_pre_bf = grad_pre.astype(jnp.bfloat16)
    grad_as = outer_sum(blocks.reshape(-1, width), grad_pre_bf)
    grad_recv = jnp.einsum(
        "scm,scbl->mbl",
        dest_hot,
        grad_pre.reshape(lon_count, capacity, B, width),
        precision=HIGHEST_PRECISION,
    )
    grad_recv_bf = grad_recv.reshape(-1, width).astype(jnp.bfloat16)
    grad_h = grad_h + by_transpose(grad_recv_bf, enc_weights[2])
    grad_ar = outer_sum(mesh_in, grad_recv_bf)
    grad_sent = (
        lax.all_to_all(
            by_transpose(grad_pre_bf, enc_weights[1])
            .reshape(lon_count, capacity, B, width)
            .astype(jnp.bfloat16),
            "lon",
            split_axis=0,
            concat_axis=0,
            tiled=True,
        )
        .astype(jnp.float32)
        .reshape(-1, width)
    )
    grid_hot = (g2m_grid[:, None] == jnp.arange(grid_blocks, dtype=jnp.int32)[None, :]).astype(
        jnp.float32
    )
    slot_grid = jnp.dot(slot_hot.astype(jnp.float32), grid_hot, precision=HIGHEST_PRECISION)
    grad_grid = jnp.einsum(
        "sg,sbl->gbl",
        slot_grid,
        grad_sent.reshape(slot_count, B, width),
        precision=HIGHEST_PRECISION,
    ).reshape(-1, width)
    grad_gz = norm_back(grad_grid, grid_norm, grid_rstd).astype(jnp.bfloat16)
    grad_e2 = outer_sum(emb_act, grad_gz)
    grad_emb = (by_transpose(grad_gz, enc_weights[0]) * swish_grad(emb_pre)).astype(jnp.bfloat16)
    grad_e1 = outer_sum(grid_x, grad_emb)
    enc_terms = jnp.stack([grad_e2, grad_as, grad_ar, grad_a2, grad_nh, grad_na, grad_n2])
    enc_shard, embed_shard = (
        lax.psum_scatter(enc_terms, ("lat", "lon"), scatter_dimension=1, tiled=True),
        lax.psum_scatter(grad_e1, ("lat", "lon"), scatter_dimension=1, tiled=True),
    )
    return (latent, grad_h, enc_shard, jnp.stack(round_shards), embed_shard)


def solution(mesh):
    return jax.shard_map(
        on_device,
        mesh=mesh,
        in_specs=(
            P(("lat", "lon"), None),
            P(("lat", "lon"), None),
            P(("lat", "lon"), None),
            P(),
            P(),
            P(),
            P(("lat", "lon")),
            P(("lat", "lon")),
            P(("lat", "lon")),
            P(("lat", "lon")),
            P(("lat", "lon"), None, None),
        ),
        out_specs=(
            P(("lat", "lon"), None),
            P(("lat", "lon"), None),
            P(None, ("lat", "lon"), None),
            P(None, None, ("lat", "lon"), None),
            P(None, ("lat", "lon")),
        ),
        check_vma=False,
    )
```

profile of v0, /device:TPU:1, one launch (start us, length us, event | category | flops | bytes accessed | tf_op | source)
XLA Modules:
  0.0 535.9 jit_solution(3815092180291655882)
XLA Ops:
  11.4 9.4 %all-to-all-start = ((s32[32,1,2]{2,1,0:T(1,128)}), s32[32,1,2]{2,1,0:T(1,128)S(1)}, u32[]{:S(2)}, u32[]{:S(2)}) async-start(s32[32,1,2]{2,1,0:T(1,128)} %bitcast.3), calls=%async_computation | async-start | bytes 32768 | tf_op jit(solution)/shard_map/all_to_all | solution.py:134
  23.4 1.6 fusion.272
  25.6 2.1 all-to-all-done
  30.1 6.0 %all-to-all-start.1 = ((bf16[32,2,32,512]{3,2,1,0:T(8,128)(2,1)}), bf16[32,2,32,512]{3,2,1,0:T(8,128)(2,1)}, u32[]{:S(2)}, u32[]{:S(2)}) async-start(bf16[32,2,32,512]{3,2,1,0:T(8,128)(2,1)} %broadcast_select_fusion), calls=%async_computation.1 | async-start | bytes 4194304 | tf_op jit(solution)/shard_map/all_to_all | solution.py:133
  49.0 2.8 gather_fusion.3
  51.9 12.0 %all-to-all-done.1 = bf16[32,2,32,512]{3,2,1,0:T(8,128)(2,1)} async-done(((bf16[32,2,32,512]{3,2,1,0:T(8,128)(2,1)}), bf16[32,2,32,512]{3,2,1,0:T(8,128)(2,1)}, u32[]{:S(2)}, u32[]{:S(2)}) %all-to-all-start.1) | async-done | bytes 2097184 | tf_op jit(solution)/shard_map/all_to_all | solution.py:133
  63.8 6.8 %multiply_convert_fusion.1 = (bf16[32,2,32,512]{3,2,1,0:T(8,128)(2,1)S(1)}, f32[32,2,32,512]{3,2,1,0:T(8,128)}) fusion(f32[32,2,32,512]{3,2,1,0:T(8,128)} %bitcast.570, pred[32,2]{1,0:T(8,128)(4,1)S(1)} %copy.178, bf16[32,2,32,512]{3,2,1,0:T(8,128)(2,1)} %all-to-all-done.1, bf16[7,512,512]{2,1,0:T(8,128)(2,1)} %param.15), kind=kOutput, calls=%fused_computation.28 | convolution fusion | flops 1081081856 | bytes 13107264 | tf_op jit(solution)/shard_map/dot_general | solution.py:28
  70.7 2.7 fusion.273
  75.4 3.8 fusion.44
  80.8 1.6 fusion.274
  83.4 2.1 fusion.127
  86.9 2.4 collective-permute-start.3
  90.6 4.2 collective-permute-start
  108.8 2.1 fusion.111
  111.6 2.1 fusion.107
  113.7 1.8 collective-permute-start.7
  116.8 4.6 collective-permute-start.4
  124.4 1.7 gather_fusion.7
  128.6 1.7 gather_fusion.6
  130.3 1.9 multiply_convert_fusion.2
  141.9 2.3 convolution_add_fusion.9
  145.8 2.2 fusion.83
  148.1 2.8 gather_fusion.8
  155.4 2.0 convolution_multiply_fusion.1
  160.0 5.1 collective-permute-start.11
  166.5 4.5 collective-permute-start.8
  178.0 2.3 convolution_add_fusion.6
  180.3 2.2 fusion.81
  182.5 1.8 gather_fusion.9
  185.2 2.1 convolution_multiply_fusion
  191.1 5.7 %collective-permute-start.15 = (bf16[1,1,32,512]{3,0,2,1:T(2,128)(2,1)S(1)}, bf16[1,1,32,512]{3,0,2,1:T(2,128)(2,1)S(1)}, u32[]{:S(2)}, u32[]{:S(2)}) collective-permute-start(bf16[1,1,32,512]{3,0,2,1:T(2,128)(2,1)S(1)} %get-tuple-element.144), channel_id=1, source_target_pairs={{1,0},{2,1},{3,2},{4,3},{5,4},{6,5},{7,6},{8,7},{9,8},{10,9},{11,1... | collective-permute-start | bytes 98312 | tf_op jit(solution)/shard_map/ppermute | solution.py:22
  198.1 4.8 collective-permute-start.12
  216.5 2.8 gather_fusion.10
  219.3 4.3 multiply_reduce_fusion
  224.6 5.2 multiply_convert_fusion
  229.8 5.8 %fusion.281 = (bf16[2048,512]{1,0:T(8,128)(2,1)S(1)}, f32[2048,512]{1,0:T(8,128)}) fusion(f32[32,2,32,512]{3,2,1,0:T(8,128)S(1)} %copy-done.83, bf16[2048,512]{1,0:T(8,128)(2,1)S(1)} %multiply_convert_fusion, bf16[7,512,512]{2,1,0:T(8,128)(2,1)} %param.15), kind=kOutput, calls=%fused_computation.468 | convolution fusion | flops 1083179008 | bytes 13107200 | tf_op jit(solution)/shard_map/dot_general | solution.py:38
  236.9 3.8 convolution_convert_fusion
  240.7 10.2 %all-to-all-start.2 = ((bf16[32,2,32,512]{3,2,1,0:T(8,128)(2,1)}), bf16[32,2,32,512]{3,2,1,0:T(8,128)(2,1)S(1)}, u32[]{:S(2)}, u32[]{:S(2)}) async-start(bf16[32,2,32,512]{3,2,1,0:T(8,128)(2,1)} %convolution_convert_fusion), calls=%async_computation.2 | async-start | bytes 4194304 | tf_op jit(solution)/shard_map/all_to_all | solution.py:260
  251.3 2.8 fusion.12
  254.1 5.9 %fusion.41 = bf16[8,32,512]{2,0,1:T(8,128)(2,1)S(1)} fusion(f32[32,2,32,512]{3,2,1,0:T(8,128)} %bitcast.569, s32[32,2]{0,1:T(2,128)S(1)} %bitcast.596), kind=kOutput, calls=%fused_computation.99 | convolution fusion | flops 100794880 | bytes 4456704 | tf_op jit(solution)/shard_map/scm,scbl->mbl/dot_general | solution.py:250
  268.9 9.9 %all-to-all-done.2 = bf16[32,2,32,512]{3,2,1,0:T(8,128)(2,1)S(1)} async-done(((bf16[32,2,32,512]{3,2,1,0:T(8,128)(2,1)}), bf16[32,2,32,512]{3,2,1,0:T(8,128)(2,1)S(1)}, u32[]{:S(2)}, u32[]{:S(2)}) %all-to-all-start.2) | async-done | bytes 2097184 | tf_op jit(solution)/shard_map/all_to_all | solution.py:260
  278.8 3.0 fusion.282
  282.8 2.5 fusion.26
  285.3 2.4 convolution_bitcast_fusion.19
  287.7 4.6 fusion.30
  293.6 2.3 fusion.29
  302.3 2.2 convolution_add_fusion.2
  304.5 218.6 %all-reduce.7.cloned.1.call-done = (f32[7,512,512]{2,1,0:T(8,128)}, f32[6,512,512]{2,1,0:T(8,128)}, f32[6,512,512]{2,1,0:T(8,128)}, f32[227,512]{1,0:T(8,128)}) async-done(((f32[7,512,512]{2,1,0:T(8,128)}, f32[6,512,512]{2,1,0:T(8,128)}, f32[6,512,512]{2,1,0:T(8,128)}, f32[227,512]{1,0:T(8,128)}), (f32[7,512,512]{2,1,0:T(8,128)}, f32[6,512,512]{2,1,0:T(8,128)}, f32[6,512,512]{2,1,0:T(8,128)}, ...) | async-done | bytes 20387856
  (362 shorter events, 114.4 us)
Async XLA Ops:
  7.2 15.1 %copy-start = (bf16[227,512]{1,0:T(8,128)(2,1)S(1)}, bf16[227,512]{1,0:T(8,128)(2,1)}, u32[]{:S(2)}) copy-start(bf16[227,512]{1,0:T(8,128)(2,1)} %param.14) | copy-start | bytes 697348
  11.4 16.3 %all-to-all-start = ((s32[32,1,2]{2,1,0:T(1,128)}), s32[32,1,2]{2,1,0:T(1,128)S(1)}, u32[]{:S(2)}, u32[]{:S(2)}) async-start(s32[32,1,2]{2,1,0:T(1,128)} %bitcast.3), calls=%async_computation | async-start | bytes 32768 | tf_op jit(solution)/shard_map/all_to_all | solution.py:134
  28.5 16.0 %copy-start.74 = (s32[16]{0:T(128)S(1)}, s32[16]{0:T(128)}, u32[]{:S(2)}) copy-start(s32[16]{0:T(128)} %param.20) | copy-start | bytes 196
  28.5 16.0 %copy-start.80 = (s32[16]{0:T(128)S(1)}, s32[16]{0:T(128)}, u32[]{:S(2)}) copy-start(s32[16]{0:T(128)} %param.19) | copy-start | bytes 196
  28.5 16.0 %copy-start.2 = (s32[40]{0:T(128)S(1)}, s32[40]{0:T(128)}, u32[]{:S(2)}) copy-start(s32[40]{0:T(128)} %param.17) | copy-start | bytes 484
  28.6 16.9 %copy-start.9 = (bf16[256,512]{1,0:T(8,128)(2,1)S(1)}, bf16[256,512]{1,0:T(8,128)(2,1)}, u32[]{:S(2)}) copy-start(bf16[256,512]{1,0:T(8,128)(2,1)} %param.12) | copy-start | bytes 786436
  30.1 33.7 %all-to-all-start.1 = ((bf16[32,2,32,512]{3,2,1,0:T(8,128)(2,1)}), bf16[32,2,32,512]{3,2,1,0:T(8,128)(2,1)}, u32[]{:S(2)}, u32[]{:S(2)}) async-start(bf16[32,2,32,512]{3,2,1,0:T(8,128)(2,1)} %broadcast_select_fusion), calls=%async_computation.1 | async-start | bytes 4194304 | tf_op jit(solution)/shard_map/all_to_all | solution.py:133
  44.5 51.7 %copy-start.73 = (s32[1024]{0:T(1024)}, s32[1024]{0:T(1024)S(1)}, u32[]{:S(2)}) copy-start(s32[1024]{0:T(1024)S(1)} %get-tuple-element.200) | copy-start | bytes 12292
  44.6 53.7 %copy-start.78 = (s32[1024]{0:T(1024)}, s32[1024]{0:T(1024)S(1)}, u32[]{:S(2)}) copy-start(s32[1024]{0:T(1024)S(1)} %get-tuple-element.201) | copy-start | bytes 12292
  48.2 27.3 %copy-start.71 = (s32[32,1,2]{0,2,1:T(2,128)}, s32[32,1,2]{0,2,1:T(2,128)S(1)}, u32[]{:S(2)}) copy-start(s32[32,1,2]{0,2,1:T(2,128)S(1)} %copy.177) | copy-start | bytes 772
  80.8 15.4 %copy-start.50 = (f32[256,512]{1,0:T(8,128)}, f32[256,512]{1,0:T(8,128)S(1)}, u32[]{:S(2)}) copy-start(f32[256,512]{1,0:T(8,128)S(1)} %convolution_add_fusion.12) | copy-start | bytes 1572868
  83.2 14.9 %copy-start.67 = (f32[256]{0:T(256)}, f32[256]{0:T(256)S(1)}, u32[]{:S(2)}) copy-start(f32[256]{0:T(256)S(1)} %add_rsqrt_fusion.5) | copy-start | bytes 3076
  86.9 9.9 %collective-permute-start.3 = (bf16[1,1,32,512]{3,2,1,0:T(8,128)(2,1)S(1)}, bf16[1,1,32,512]{3,2,1,0:T(8,128)(2,1)S(1)}, u32[]{:S(2)}, u32[]{:S(2)}) collective-permute-start(bf16[1,1,32,512]{3,2,1,0:T(8,128)(2,1)S(1)} %get-tuple-element.159), channel_id=1, source_target_pairs={{1,0},{2,1},{3,2},{4,3},{5,4},{6,5},{7,6},{8,7},{9,8},{10,9},{11,1... | collective-permute-start | bytes 98312 | tf_op jit(solution)/shard_map/ppermute | solution.py:22
  89.3 7.5 %collective-permute-start.2 = (bf16[1,1,32,512]{3,2,1,0:T(8,128)(2,1)S(1)}, bf16[1,1,32,512]{3,2,1,0:T(8,128)(2,1)S(1)}, u32[]{:S(2)}, u32[]{:S(2)}) collective-permute-start(bf16[1,1,32,512]{3,2,1,0:T(8,128)(2,1)S(1)} %get-tuple-element.160), channel_id=1, source_target_pairs={{0,1},{1,2},{2,3},{3,4},{4,5},{5,6},{6,7},{7,8},{8,9},{9,10},{10,1... | collective-permute-start | bytes 98312 | tf_op jit(solution)/shard_map/ppermute | solution.py:21
  89.3 7.5 %collective-permute-start.1 = (bf16[1,1,32,512]{3,2,1,0:T(8,128)(2,1)S(1)}, bf16[1,1,32,512]{3,2,1,0:T(8,128)(2,1)S(1)}, u32[]{:S(2)}, u32[]{:S(2)}) collective-permute-start(bf16[1,1,32,512]{3,2,1,0:T(8,128)(2,1)S(1)} %get-tuple-element.161), channel_id=1, source_target_pairs={{32,0},{64,32},{96,64},{33,1},{65,33},{97,65},{34,2},{66,34},{98,6... | collective-permute-start | bytes 98312 | tf_op jit(solution)/shard_map/ppermute | solution.py:22
  90.6 6.2 %collective-permute-start = (bf16[1,1,32,512]{3,2,1,0:T(8,128)(2,1)S(1)}, bf16[1,1,32,512]{3,2,1,0:T(8,128)(2,1)S(1)}, u32[]{:S(2)}, u32[]{:S(2)}) collective-permute-start(bf16[1,1,32,512]{3,2,1,0:T(8,128)(2,1)S(1)} %get-tuple-element.158), channel_id=1, source_target_pairs={{0,32},{32,64},{64,96},{1,33},{33,65},{65,97},{2,34},{34,66},{66,9... | collective-permute-start | bytes 98312 | tf_op jit(solution)/shard_map/ppermute | solution.py:21
  106.8 14.7 %copy-start.53 = (f32[256,512]{1,0:T(8,128)}, f32[256,512]{1,0:T(8,128)S(1)}, u32[]{:S(2)}) copy-start(f32[256,512]{1,0:T(8,128)S(1)} %convolution_add_fusion.11) | copy-start | bytes 1572868
  108.4 15.9 %copy-start.7 = (f32[256,512]{1,0:T(8,128)}, f32[256,512]{1,0:T(8,128)S(1)}, u32[]{:S(2)}) copy-start(f32[256,512]{1,0:T(8,128)S(1)} %get-tuple-element.185) | copy-start | bytes 1572868
  108.7 17.4 %copy-start.69 = (f32[256]{0:T(256)}, f32[256]{0:T(256)S(1)}, u32[]{:S(2)}) copy-start(f32[256]{0:T(256)S(1)} %add_rsqrt_fusion.4) | copy-start | bytes 3076
  113.7 12.3 %collective-permute-start.7 = (bf16[1,1,32,512]{3,2,1,0:T(8,128)(2,1)}, bf16[1,1,32,512]{3,2,1,0:T(8,128)(2,1)}, u32[]{:S(2)}, u32[]{:S(2)}) collective-permute-start(bf16[1,1,32,512]{3,2,1,0:T(8,128)(2,1)} %get-tuple-element.155), channel_id=1, source_target_pairs={{1,0},{2,1},{3,2},{4,3},{5,4},{6,5},{7,6},{8,7},{9,8},{10,9},{11,1... | collective-permute-start | bytes 98312 | tf_op jit(solution)/shard_map/ppermute | solution.py:22
  115.5 10.5 %collective-permute-start.6 = (bf16[1,1,32,512]{3,2,1,0:T(8,128)(2,1)S(1)}, bf16[1,1,32,512]{3,2,1,0:T(8,128)(2,1)}, u32[]{:S(2)}, u32[]{:S(2)}) collective-permute-start(bf16[1,1,32,512]{3,2,1,0:T(8,128)(2,1)S(1)} %get-tuple-element.156), channel_id=1, source_target_pairs={{0,1},{1,2},{2,3},{3,4},{4,5},{5,6},{6,7},{7,8},{8,9},{9,10},{10,1... | collective-permute-start | bytes 98312 | tf_op jit(solution)/shard_map/ppermute | solution.py:21
  115.5 10.5 %collective-permute-start.5 = (bf16[1,1,32,512]{3,2,1,0:T(8,128)(2,1)S(1)}, bf16[1,1,32,512]{3,2,1,0:T(8,128)(2,1)}, u32[]{:S(2)}, u32[]{:S(2)}) collective-permute-start(bf16[1,1,32,512]{3,2,1,0:T(8,128)(2,1)S(1)} %get-tuple-element.157), channel_id=1, source_target_pairs={{32,0},{64,32},{96,64},{33,1},{65,33},{97,65},{34,2},{66,34},{98,6... | collective-permute-start | bytes 98312 | tf_op jit(solution)/shard_map/ppermute | solution.py:22
  116.8 9.3 %collective-permute-start.4 = (bf16[1,1,32,512]{3,2,1,0:T(8,128)(2,1)S(1)}, bf16[1,1,32,512]{3,2,1,0:T(8,128)(2,1)}, u32[]{:S(2)}, u32[]{:S(2)}) collective-permute-start(bf16[1,1,32,512]{3,2,1,0:T(8,128)(2,1)S(1)} %get-tuple-element.154), channel_id=1, source_target_pairs={{0,32},{32,64},{64,96},{1,33},{33,65},{65,97},{2,34},{34,66},{66,9... | collective-permute-start | bytes 98312 | tf_op jit(solution)/shard_map/ppermute | solution.py:21
  155.4 15.8 %copy-start.16 = (bf16[512,512]{1,0:T(8,128)(2,1)}, bf16[512,512]{1,0:T(8,128)(2,1)S(1)}, u32[]{:S(2)}) copy-start(bf16[512,512]{1,0:T(8,128)(2,1)S(1)} %fusion.67) | copy-start | bytes 1572868
  155.4 17.0 %copy-start.77 = (s32[1,4,1]{1,2,0:T(1,128)S(1)}, s32[1,4,1]{1,2,0:T(1,128)}, u32[]{:S(2)}) copy-start(s32[1,4,1]{1,2,0:T(1,128)} %param.21) | copy-start | bytes 52
  157.5 15.7 %copy-start.40 = (f32[256,512]{1,0:T(8,128)S(1)}, f32[256,512]{1,0:T(8,128)}, u32[]{:S(2)}) copy-start(f32[256,512]{1,0:T(8,128)} %convolution_add_fusion.9) | copy-start | bytes 1572868
  157.5 17.2 %copy-start.8 = (f32[256,512]{1,0:T(8,128)S(1)}, f32[256,512]{1,0:T(8,128)}, u32[]{:S(2)}) copy-start(f32[256,512]{1,0:T(8,128)} %copy-done.7) | copy-start | bytes 1572868
  157.5 17.2 %copy-start.70 = (f32[256]{0:T(256)S(1)}, f32[256]{0:T(256)}, u32[]{:S(2)}) copy-start(f32[256]{0:T(256)} %copy-done.69) | copy-start | bytes 3076
  160.0 11.2 %collective-permute-start.11 = (bf16[1,1,32,512]{3,0,2,1:T(2,128)(2,1)S(1)}, bf16[1,1,32,512]{3,0,2,1:T(2,128)(2,1)S(1)}, u32[]{:S(2)}, u32[]{:S(2)}) collective-permute-start(bf16[1,1,32,512]{3,0,2,1:T(2,128)(2,1)S(1)} %get-tuple-element.150), channel_id=1, source_target_pairs={{1,0},{2,1},{3,2},{4,3},{5,4},{6,5},{7,6},{8,7},{9,8},{10,9},{11,1... | collective-permute-start | bytes 98312 | tf_op jit(solution)/shard_map/ppermute | solution.py:22
  165.1 6.1 %collective-permute-start.10 = (bf16[1,1,32,512]{3,0,2,1:T(2,128)(2,1)S(1)}, bf16[1,1,32,512]{3,0,2,1:T(2,128)(2,1)S(1)}, u32[]{:S(2)}, u32[]{:S(2)}) collective-permute-start(bf16[1,1,32,512]{3,0,2,1:T(2,128)(2,1)S(1)} %get-tuple-element.149), channel_id=1, source_target_pairs={{0,1},{1,2},{2,3},{3,4},{4,5},{5,6},{6,7},{7,8},{8,9},{9,10},{10,1... | collective-permute-start | bytes 98312 | tf_op jit(solution)/shard_map/ppermute | solution.py:21
  165.2 6.4 %collective-permute-start.9 = (bf16[1,1,32,512]{3,0,2,1:T(2,128)(2,1)S(1)}, bf16[1,1,32,512]{3,0,2,1:T(2,128)(2,1)S(1)}, u32[]{:S(2)}, u32[]{:S(2)}) collective-permute-start(bf16[1,1,32,512]{3,0,2,1:T(2,128)(2,1)S(1)} %get-tuple-element.151), channel_id=1, source_target_pairs={{32,0},{64,32},{96,64},{33,1},{65,33},{97,65},{34,2},{66,34},{98,6... | collective-permute-start | bytes 98312 | tf_op jit(solution)/shard_map/ppermute | solution.py:22
  166.5 5.4 %collective-permute-start.8 = (bf16[1,1,32,512]{3,0,2,1:T(2,128)(2,1)S(1)}, bf16[1,1,32,512]{3,0,2,1:T(2,128)(2,1)S(1)}, u32[]{:S(2)}, u32[]{:S(2)}) collective-permute-start(bf16[1,1,32,512]{3,0,2,1:T(2,128)(2,1)S(1)} %get-tuple-element.148), channel_id=1, source_target_pairs={{0,32},{32,64},{64,96},{1,33},{33,65},{65,97},{2,34},{34,66},{66,9... | collective-permute-start | bytes 98312 | tf_op jit(solution)/shard_map/ppermute | solution.py:21
  185.2 17.7 %copy-start.31 = (bf16[8,32,512]{2,1,0:T(8,128)(2,1)S(1)}, bf16[8,32,512]{2,1,0:T(8,128)(2,1)}, u32[]{:S(2)}) copy-start(bf16[8,32,512]{2,1,0:T(8,128)(2,1)} %copy-done.30) | copy-start | bytes 786436
  187.2 17.0 %copy-start.17 = (bf16[512,512]{1,0:T(8,128)(2,1)S(1)}, bf16[512,512]{1,0:T(8,128)(2,1)}, u32[]{:S(2)}) copy-start(bf16[512,512]{1,0:T(8,128)(2,1)} %copy-done.16) | copy-start | bytes 1572868
  187.2 17.0 %copy-start.45 = (bf16[512,512]{1,0:T(8,128)(2,1)S(1)}, bf16[512,512]{1,0:T(8,128)(2,1)}, u32[]{:S(2)}) copy-start(bf16[512,512]{1,0:T(8,128)(2,1)} %get-tuple-element.139) | copy-start | bytes 1572868
  188.5 17.2 %copy-start.23 = (bf16[256,512]{1,0:T(8,128)(2,1)S(1)}, bf16[256,512]{1,0:T(8,128)(2,1)}, u32[]{:S(2)}) copy-start(bf16[256,512]{1,0:T(8,128)(2,1)} %copy-done.22) | copy-start | bytes 786436
  188.5 18.5 %copy-start.29 = (bf16[8,32,512]{2,1,0:T(8,128)(2,1)S(1)}, bf16[8,32,512]{2,1,0:T(8,128)(2,1)}, u32[]{:S(2)}) copy-start(bf16[8,32,512]{2,1,0:T(8,128)(2,1)} %copy-done.28) | copy-start | bytes 786436
  191.1 17.4 %collective-permute-start.15 = (bf16[1,1,32,512]{3,0,2,1:T(2,128)(2,1)S(1)}, bf16[1,1,32,512]{3,0,2,1:T(2,128)(2,1)S(1)}, u32[]{:S(2)}, u32[]{:S(2)}) collective-permute-start(bf16[1,1,32,512]{3,0,2,1:T(2,128)(2,1)S(1)} %get-tuple-element.144), channel_id=1, source_target_pairs={{1,0},{2,1},{3,2},{4,3},{5,4},{6,5},{7,6},{8,7},{9,8},{10,9},{11,1... | collective-permute-start | bytes 98312 | tf_op jit(solution)/shard_map/ppermute | solution.py:22
  196.8 11.7 %collective-permute-start.14 = (bf16[1,1,32,512]{3,0,2,1:T(2,128)(2,1)S(1)}, bf16[1,1,32,512]{3,0,2,1:T(2,128)(2,1)S(1)}, u32[]{:S(2)}, u32[]{:S(2)}) collective-permute-start(bf16[1,1,32,512]{3,0,2,1:T(2,128)(2,1)S(1)} %get-tuple-element.143), channel_id=1, source_target_pairs={{0,1},{1,2},{2,3},{3,4},{4,5},{5,6},{6,7},{7,8},{8,9},{9,10},{10,1... | collective-permute-start | bytes 98312 | tf_op jit(solution)/shard_map/ppermute | solution.py:21
  196.8 12.1 %collective-permute-start.13 = (bf16[1,1,32,512]{3,0,2,1:T(2,128)(2,1)S(1)}, bf16[1,1,32,512]{3,0,2,1:T(2,128)(2,1)S(1)}, u32[]{:S(2)}, u32[]{:S(2)}) collective-permute-start(bf16[1,1,32,512]{3,0,2,1:T(2,128)(2,1)S(1)} %get-tuple-element.145), channel_id=1, source_target_pairs={{32,0},{64,32},{96,64},{33,1},{65,33},{97,65},{34,2},{66,34},{98,6... | collective-permute-start | bytes 98312 | tf_op jit(solution)/shard_map/ppermute | solution.py:22
  198.1 10.8 %collective-permute-start.12 = (bf16[1,1,32,512]{3,0,2,1:T(2,128)(2,1)S(1)}, bf16[1,1,32,512]{3,0,2,1:T(2,128)(2,1)S(1)}, u32[]{:S(2)}, u32[]{:S(2)}) collective-permute-start(bf16[1,1,32,512]{3,0,2,1:T(2,128)(2,1)S(1)} %get-tuple-element.142), channel_id=1, source_target_pairs={{0,32},{32,64},{64,96},{1,33},{33,65},{65,97},{2,34},{34,66},{66,9... | collective-permute-start | bytes 98312 | tf_op jit(solution)/shard_map/ppermute | solution.py:21
  236.9 14.3 %copy-start.49 = (bf16[256,512]{1,0:T(8,128)(2,1)S(1)}, bf16[256,512]{1,0:T(8,128)(2,1)}, u32[]{:S(2)}) copy-start(bf16[256,512]{1,0:T(8,128)(2,1)} %param.13) | copy-start | bytes 786436
  240.7 13.4 %copy-start.72 = (s32[32,1,2]{0,2,1:T(2,128)S(1)}, s32[32,1,2]{0,2,1:T(2,128)}, u32[]{:S(2)}) copy-start(s32[32,1,2]{0,2,1:T(2,128)} %copy-done.71) | copy-start | bytes 772
  240.7 38.1 %all-to-all-start.2 = ((bf16[32,2,32,512]{3,2,1,0:T(8,128)(2,1)}), bf16[32,2,32,512]{3,2,1,0:T(8,128)(2,1)S(1)}, u32[]{:S(2)}, u32[]{:S(2)}) async-start(bf16[32,2,32,512]{3,2,1,0:T(8,128)(2,1)} %convolution_convert_fusion), calls=%async_computation.2 | async-start | bytes 4194304 | tf_op jit(solution)/shard_map/all_to_all | solution.py:260
  251.0 272.1 %all-reduce.7.cloned.1.call-start = ((), (), s32[]{:S(2)}) async-start(), calls=%async_computation.3 | async-start | bytes 40796160
  263.4 15.4 %copy-start.79 = (f32[64,8,1]{0,1,2:T(8,128)S(1)}, f32[64,8,1]{0,1,2:T(8,128)}, u32[]{:S(2)}) copy-start(f32[64,8,1]{0,1,2:T(8,128)} %convolution_bitcast_fusion.20) | copy-start | bytes 6148
  266.2 16.0 %copy-start.66 = (f32[256]{0:T(256)S(1)}, f32[256]{0:T(256)}, u32[]{:S(2)}) copy-start(f32[256]{0:T(256)} %copy-done.65) | copy-start | bytes 3076
  299.9 228.9 %copy-start.1 = (bf16[227,512]{1,0:T(8,128)(2,1)S(1)}, bf16[227,512]{1,0:T(8,128)(2,1)}, u32[]{:S(2)}) copy-start(bf16[227,512]{1,0:T(8,128)(2,1)} %param.14) | copy-start | bytes 697348
  (56 other events, 269.5 us)
Sparse Core Ops, SparseCore 0:
  300.0 223.0 all-reduce.6
where the time goes:
time: 541 us; the launch traced here: 536 us
  waiting for transfers between devices  243 us (45%)
  matrix products  135 us (25%)
  starting transfers between devices  64.2 us (12%)
  other arithmetic  35.2 us (7%)
  local copies, waits for them, and re-layouts  35 us (6%)
  between operations  23.8 us (4%)
    unnamed x2, waiting for transfers between devices  219 us
    dot_general x22, matrix products, matmul(): return jnp.dot(first_op, second_op, preferred_element_type=jnp.float32)  40.3 us
    dot_general x18, matrix products, by_transpose(): lax.dot_general(grad_in, weight, (((1,), (1,)), ((), ())), preferred_elem...  38.1 us
    dot_general x20, matrix products, outer_sum(): lax.dot_general(first_op, second_op, (((0,), (0,)), ((), ())), preferred_...  34.6 us
    ppermute x8, starting transfers between devices, extended(): after = lax.ppermute(leading, axis, down)  20.2 us
    ppermute x8, starting transfers between devices, extended(): before = lax.ppermute(last, axis, up)  18.1 us
    all_to_all x1, waiting for transfers between devices, on_device(): lax.all_to_all(send_blocks, 'lon', split_axis=0, concat_axis=0, tiled=True)  12 us
  transfers between devices with their start and end apart: 20, of which 5 were waited for; matrix products, arithmetic and copies ran while one was open for 9% of the time, Pallas kernels for 0%

commit v1 on v0

v1 whole, which is shorter than its diff:
```python
import functools

import jax
import jax.numpy as jnp
from jax import lax
from jax.experimental import pallas as pl
from jax.experimental.pallas import tpu as pltpu
from jax.sharding import PartitionSpec as P

B = 32
L = 512
T = 256
MB = 8
ROUNDS = 2
EPSILON = 1e-05
BF = jnp.bfloat16
F32 = jnp.float32
MESH = pl.DeviceIdType.MESH
HALF = L // 2
OPPOSITE = (1, 0, 3, 2)


def mm(a, b):
    return jnp.dot(a, b, preferred_element_type=F32)


def mt(a, b):
    return lax.dot_general(a, b, (((1,), (1,)), ((), ())), preferred_element_type=F32)


def tm(a, b):
    return lax.dot_general(a, b, (((0,), (0,)), ((), ())), preferred_element_type=F32)


def sigmoid(x):
    return 0.5 * jnp.tanh(0.5 * x) + 0.5


def swish(x):
    return x * sigmoid(x)


def swish_grad(x):
    s = sigmoid(x)
    return s * (1.0 + x * (1.0 - s))


def norm_rows(z):
    centred = z - jnp.mean(z, axis=-1, keepdims=True)
    r = lax.rsqrt(jnp.mean(centred * centred, axis=-1, keepdims=True) + EPSILON)
    return centred * r, r


def norm_back(g, y, r):
    return r * (
        g - jnp.mean(g, axis=-1, keepdims=True) - y * jnp.mean(g * y, axis=-1, keepdims=True)
    )


def iota(shape, dim):
    return lax.broadcasted_iota(jnp.int32, shape, dim)


def wide(r):
    return jnp.broadcast_to(r, (r.shape[0], 128))


def one_hot_rows(scalars, columns):
    col = iota((B, columns), 1)
    diag = (col & (B - 1)) == iota((B, columns), 0)
    block = col >> 5
    return [jnp.where(diag & (block == s), 1.0, 0.0).astype(BF) for s in scalars]


class Scatter:
    def __init__(self, cfg, where, refs, send, recv, base, rows):
        self.cfg, self.where, self.refs, self.rows = cfg, where, refs, rows
        self.send, self.recv, self.base = send, recv, base
        self.flying = []

    def copy(self, src, dst, index, device):
        c = pltpu.make_async_remote_copy(
            src_ref=src,
            dst_ref=dst,
            send_sem=self.send.at[self.base + index],
            recv_sem=self.recv.at[self.base + index],
            device_id=device,
            device_id_type=MESH,
        )
        c.start()
        self.flying.append(c)

    def wait(self):
        for c in self.flying:
            c.wait()
        self.flying = []

    def cols(self, which):
        return pl.ds(pl.multiple_of(which * HALF, HALF), HALF)

    def start_core(self):
        w = self.where
        own, crecv = self.refs.own, self.refs.crecv
        self.copy(own.at[:, :, self.cols(1 - w.core)], crecv, 0, (w.lat, w.sibling))

    def start_y(self):
        w, (ny, nz, nx) = self.where, self.cfg
        own, crecv, yrecv = self.refs.own, self.refs.crecv, self.refs.yrecv
        self.wait()
        mine = self.cols(w.core)
        step = 4

        def body(i, _):
            at = pl.ds(i * step, step)
            own[at, :, mine] = (own[at, :, mine].astype(F32) + crecv[at].astype(F32)).astype(BF)
            return 0

        lax.fori_loop(0, ny * nz * nx // step, body, 0)
        for j in range(1, ny):
            to = lax.rem(w.lat + j, ny)
            self.copy(
                own.at[pl.ds(to * nz * nx, nz * nx), :, mine],
                yrecv.at[j - 1],
                j,
                (to, w.lon),
            )

    def start_z(self):
        w, (ny, nz, nx) = self.where, self.cfg
        own, yrecv, zrecv = self.refs.own, self.refs.yrecv, self.refs.zrecv
        self.wait()
        mine = self.cols(w.core)
        base = w.lat * nz * nx

        def body(i, _):
            total = own[base + i, :, mine].astype(F32)
            for j in range(ny - 1):
                total = total + yrecv[j, i].astype(F32)
            own[base + i, :, mine] = total.astype(BF)
            return 0

        lax.fori_loop(0, nz * nx, body, 0)
        for j in range(1, nz):
            to = lax.rem(w.z + j, nz)
            self.copy(
                own.at[pl.ds(base + to * nx, nx), :, mine],
                zrecv.at[j - 1],
                ny - 1 + j,
                (w.lat, (to * nx + w.x) * 2 + w.core),
            )

    def start_x(self):
        w, (ny, nz, nx) = self.where, self.cfg
        own, zrecv, xrecv = self.refs.own, self.refs.zrecv, self.refs.xrecv
        self.wait()
        mine = self.cols(w.core)
        base = (w.lat * nz + w.z) * nx

        def body(i, _):
            total = own[base + i, :, mine].astype(F32)
            for j in range(nz - 1):
                total = total + zrecv[j, i].astype(F32)
            own[base + i, :, mine] = total.astype(BF)
            return 0

        lax.fori_loop(0, nx, body, 0)
        for j in range(1, nx):
            to = lax.rem(w.x + j, nx)
            self.copy(
                own.at[base + to, :, mine],
                xrecv.at[j - 1],
                ny - 1 + nz - 1 + j,
                (w.lat, (w.z * nx + to) * 2 + w.core),
            )

    def start_swap(self):
        w, (ny, nz, nx) = self.where, self.cfg
        own, xrecv = self.refs.own, self.refs.xrecv
        fin, swap = self.refs.fin, self.refs.swap
        self.wait()
        total = own[(w.lat * nz + w.z) * nx + w.x, :, self.cols(w.core)].astype(F32)
        for j in range(nx - 1):
            total = total + xrecv[j].astype(F32)
        fin[...] = total
        self.copy(fin, swap, ny + nz + nx - 2, (w.lat, w.sibling))

    def finish(self):
        w, (ny, nz, nx) = self.where, self.cfg
        fin, swap = self.refs.fin, self.refs.swap
        self.wait()
        per = L // (ny * nz * nx)
        mine, other = fin[...], swap[...]
        left = jnp.where(w.core == 0, mine, other)
        right = jnp.where(w.core == 0, other, mine)
        keep = []
        for k in range(self.rows // per):
            pair = []
            for side in (left, right):
                rows = side[k * per : (k + 1) * per]
                pair.append(jnp.where(w.core == 0, rows[: per // 2], rows[per // 2 :]))
            keep.append(pair)
        return keep


class Space:
    pass


def scratch_plan(cfg, n, slots, edges):
    ny, nz, nx = cfg
    chips = ny * nz * nx
    per = L // chips
    rows = slots * B
    ids = slots * 8
    v = Space()

    def vm(*shape, dtype=BF):
        return pltpu.VMEM(shape, dtype)

    v.encw = vm(7, L, L)
    v.procw = vm(ROUNDS, 6, L, L)
    v.emb_pre = vm(T, L, dtype=F32)
    v.emb_act = vm(T, L)
    v.grid_norm = vm(T, L, dtype=F32)
    v.grid_r = vm(T, 128, dtype=F32)
    v.G = vm(rows, T)
    v.sendbuf = vm(rows, L)
    v.recvbuf = vm(rows, L)
    v.backbuf = vm(rows, L)
    v.ids_send = vm(ids, 128)
    v.ids_recv = vm(ids, 128)
    v.Pm = vm(rows, T)
    v.recv_proj = vm(T, L)
    v.g_pre = vm(rows, L)
    v.g_act = vm(rows, L)
    v.g_msg = vm(rows, L)
    v.g_r = vm(rows, 128, dtype=F32)
    v.acc = vm(T, L, dtype=F32)
    v.gsum = vm(T, L)
    v.u_s = []
    v.u_gate = []
    v.u_hid = []
    v.u_y = []
    v.u_r = []
    for u in range(ROUNDS + 1):
        v.u_s.append(vm(T, L))
        v.u_gate.append(vm(T, L))
        v.u_hid.append(vm(T, L))
        v.u_y.append(vm(T, L))
        v.u_r.append(vm(T, 128, dtype=F32))
    v.dz = vm(T, L)
    v.dgate = vm(T, L)
    v.drecv = vm(T, L)
    v.dproj = vm(T, L)
    v.gh = vm(T, L, dtype=F32)
    v.Ps = vm(edges * B, T + 4 * B)
    v.Pr = vm(edges * B, T)
    v.H = vm(4 * B, T)
    v.ext = []
    v.hsend = []
    v.bsend = []
    v.brecv = []
    v.e_pre = []
    v.e_act = []
    v.e_msg = []
    v.e_r = []
    for r in range(ROUNDS):
        v.ext.append(vm(T + 4 * B, L))
        v.hsend.append(vm(4 * B, L))
        v.bsend.append(vm(4 * B, L))
        v.brecv.append(vm(4 * B, L))
        v.e_pre.append(vm(edges * B, L))
        v.e_act.append(vm(edges * B, L))
        v.e_msg.append(vm(edges * B, L))
        v.e_r.append(vm(edges * B, 128, dtype=F32))
    v.own = []
    v.crecv = []
    v.yrecv = []
    v.zrecv = []
    v.xrecv = []
    v.fin = []
    v.swap = []
    for p, count in enumerate((6, 6, 6, 2)):
        r = count * per
        v.own.append(vm(chips, r, L))
        if p < 2:
            v.crecv.append(vm(chips, r, HALF))
        v.yrecv.append(vm(ny - 1, nz * nx, r, HALF))
        v.zrecv.append(vm(nz - 1, nx, r, HALF))
        v.xrecv.append(vm(nx - 1, r, HALF))
        v.fin.append(vm(r, HALF, dtype=F32))
        v.swap.append(vm(r, HALF, dtype=F32))
    hops = ny + nz + nx - 1
    dma = pltpu.SemaphoreType.DMA
    v.w_sem = dma((2,))
    v.ids_ss, v.ids_rs = dma((n,)), dma((n,))
    v.fwd_ss, v.fwd_rs = dma((n,)), dma((n,))
    v.back_ss, v.back_rs = dma((n,)), dma((n,))
    v.halo_ss, v.halo_rs = dma((8 * ROUNDS,)), dma((8 * ROUNDS,))
    v.rs_ss, v.rs_rs = dma((4 * hops,)), dma((4 * hops,))
    return v


def leaves(plan):
    return [x for v in vars(plan).values() for x in (v if isinstance(v, list) else [v])]


def bind(plan, refs):
    rest, out = iter(refs), Space()
    for name, v in vars(plan).items():
        setattr(out, name, [next(rest) for _ in v] if isinstance(v, list) else next(rest))
    return out


def kernel(
    cfg,
    n,
    cap,
    plan,
    gx,
    mesh_in,
    mgrad,
    emb,
    encw_hbm,
    procw_hbm,
    mrow,
    mcol,
    grow,
    msend,
    mrecv,
    hidx,
    out_lat,
    out_gin,
    out_enc,
    out_proc,
    out_emb,
    *scratch,
):
    s = bind(plan, scratch)
    ny, nz, nx = cfg
    chips = ny * nz * nx
    per = L // chips
    slots = n * cap
    tiles = slots * B // T
    ppt = T // (cap * B)
    edges = msend.shape[0]
    hops = ny + nz + nx - 1

    w = Space()
    w.lat, w.lon = lax.axis_index("lat"), lax.axis_index("lon")
    w.core = lax.rem(w.lon, 2)
    w.sibling = w.lon + 1 - 2 * w.core
    w.x = lax.rem(w.lon // 2, nx)
    w.z = w.lon // (2 * nx)
    me = w.lon

    enc_copy = pltpu.make_async_copy(encw_hbm, s.encw, s.w_sem.at[0])
    proc_copy = pltpu.make_async_copy(procw_hbm, s.procw, s.w_sem.at[1])
    enc_copy.start()
    proc_copy.start()

    barrier = pltpu.get_barrier_semaphore()

    def greet(k, _):
        pl.semaphore_signal(
            barrier, inc=1, device_id=(w.lat, lax.rem(me + k, n)), device_id_type=MESH
        )
        return 0

    lax.fori_loop(1, n, greet, 0)
    for j in range(1, ny):
        pl.semaphore_signal(
            barrier, inc=1, device_id=(lax.rem(w.lat + j, ny), me), device_id_type=MESH
        )

    own_c = (mcol[...] >> 3) & (n - 1)
    own_r = (mrow[...] >> 3) & (n - 1)
    count = mrow.shape[1]
    before = (own_c == own_r) & (iota((count, count), 0) < iota((count, count), 1))
    rank = jnp.sum(jnp.where(before, 1.0, 0.0), axis=0, keepdims=True)
    slot = own_r.astype(F32) * cap + rank
    hot = iota((slots, count), 0).astype(F32) == slot
    block = jnp.sum(jnp.where(hot, grow[...].astype(F32) + 1.0, 0.0), axis=1, keepdims=True) - 1.0
    dest = (
        jnp.sum(jnp.where(hot, (mrow[...] & (MB - 1)).astype(F32) + 1.0, 0.0), axis=1, keepdims=True)
        - 1.0
    )
    spread = (iota((slots * 8, slots), 0) >> 3) == iota((slots * 8, slots), 1)
    s.ids_send[...] = mm(
        jnp.where(spread, 1.0, 0.0).astype(BF),
        jnp.broadcast_to(dest, (slots, 128)).astype(BF),
    ).astype(BF)
    pl.semaphore_wait(barrier, n - 1 + ny - 1)

    def row_copy(src, dst, size, ss, rs, to):
        return pltpu.make_async_remote_copy(
            src_ref=src.at[pl.ds(pl.multiple_of(to * size, size), size)],
            dst_ref=dst.at[pl.ds(pl.multiple_of(me * size, size), size)],
            send_sem=ss.at[to],
            recv_sem=rs.at[me],
            device_id=(w.lat, to),
            device_id_type=MESH,
        )

    def row_wait(src, dst, size, ss, rs, frm):
        return pltpu.make_async_remote_copy(
            src_ref=src.at[pl.ds(pl.multiple_of(frm * size, size), size)],
            dst_ref=dst.at[pl.ds(pl.multiple_of(frm * size, size), size)],
            send_sem=ss.at[frm],
            recv_sem=rs.at[frm],
            device_id=(w.lat, frm),
            device_id_type=MESH,
        )

    ids_args = (s.ids_send, s.ids_recv, cap * 8, s.ids_ss, s.ids_rs)
    fwd_args = (s.sendbuf, s.recvbuf, cap * B, s.fwd_ss, s.fwd_rs)
    back_args = (s.sendbuf, s.backbuf, cap * B, s.back_ss, s.back_rs)

    def send_all(args):
        def body(k, _):
            row_copy(*args, lax.rem(me + k, n)).start()
            return 0

        lax.fori_loop(1, n, body, 0)

    def sent_all(args):
        def body(k, _):
            row_wait(*args, lax.rem(me + k, n)).wait_send()
            return 0

        lax.fori_loop(1, n, body, 0)

    def keep_own(args):
        src, dst, size = args[:3]
        at = pl.ds(pl.multiple_of(me * size, size), size)
        dst[at] = src[at]

    send_all(ids_args)
    keep_own(ids_args)

    col = iota((T, T), 1)
    diag = (col & (B - 1)) == (iota((T, T), 0) & (B - 1))
    col_block = (col >> 5).astype(F32)
    block_b = jnp.broadcast_to(block, (slots, T)).astype(BF)

    def pick_grid(t, _):
        expand = ((iota((T, slots), 0) + t * T) >> 5) == iota((T, slots), 1)
        value = mm(jnp.where(expand, 1.0, 0.0).astype(BF), block_b)
        s.G[pl.ds(pl.multiple_of(t * T, T), T)] = jnp.where(
            diag & (value == col_block), 1.0, 0.0
        ).astype(BF)
        return 0

    lax.fori_loop(0, tiles, pick_grid, 0)

    emb_pre = mm(gx[...], emb[...])
    s.emb_pre[...] = emb_pre
    emb_act = swish(emb_pre).astype(BF)
    s.emb_act[...] = emb_act
    enc_copy.wait()
    encw = s.encw
    grid_norm, grid_r = norm_rows(mm(emb_act, encw[0]))
    s.grid_norm[...] = grid_norm
    s.grid_r[...] = wide(grid_r)
    s.gsum[...] = grid_norm.astype(BF)

    def fill(t, _):
        at = pl.ds(pl.multiple_of(t * T, T), T)
        s.sendbuf[at] = mm(s.G[at], s.gsum[...]).astype(BF)
        return 0

    lax.fori_loop(0, tiles, fill, 0)
    send_all(fwd_args)
    keep_own(fwd_args)

    s.recv_proj[...] = mm(mesh_in[...], encw[2]).astype(BF)
    for e in range(edges):
        (pick,) = one_hot_rows([msend[e]], T + 4 * B)
        s.Ps[pl.ds(e * B, B)] = pick
        (pick,) = one_hot_rows([mrecv[e]], T)
        s.Pr[pl.ds(e * B, B)] = pick
    for k in range(4):
        (pick,) = one_hot_rows([hidx[k]], T)
        s.H[pl.ds(k * B, B)] = pick

    def ids_wait(k, _):
        row_wait(*ids_args, lax.rem(me + k, n)).wait_recv()
        return 0

    lax.fori_loop(1, n, ids_wait, 0)
    id_rows = ppt * cap * 8
    id_pick = iota((T, id_rows), 1) == ((iota((T, id_rows), 0) >> 5) << 3)
    id_pick = jnp.where(id_pick, 1.0, 0.0).astype(BF)

    def pick_mesh(t, _):
        value = mm(id_pick, s.ids_recv[pl.ds(pl.multiple_of(t * id_rows, id_rows), id_rows)])
        value = jnp.concatenate([value, value], axis=1)
        s.Pm[pl.ds(pl.multiple_of(t * T, T), T)] = jnp.where(
            diag & (value == col_block), 1.0, 0.0
        ).astype(BF)
        return 0

    lax.fori_loop(0, tiles, pick_mesh, 0)
    s.acc[...] = jnp.zeros((T, L), F32)

    def edge_tile(i, _):
        t = lax.rem(me // ppt + tiles - i, tiles)
        for q in range(ppt):
            frm = t * ppt + q

            @pl.when(frm != me)
            def _():
                row_wait(*fwd_args, frm).wait_recv()

        at = pl.ds(pl.multiple_of(t * T, T), T)
        pick = s.Pm[at]
        pre = mm(s.recvbuf[at], encw[1]) + mm(pick, s.recv_proj[...])
        s.g_pre[at] = pre.astype(BF)
        act = swish(pre).astype(BF)
        s.g_act[at] = act
        msg, r = norm_rows(mm(act, encw[3]))
        s.g_r[at] = wide(r)
        msg = msg.astype(BF)
        s.g_msg[at] = msg
        s.acc[...] += tm(pick, msg)
        return 0

    lax.fori_loop(0, tiles, edge_tile, 0)

    def update(u, h, total, wh, wa, wo):
        sb = total.astype(BF)
        s.u_s[u][...] = sb
        gate = mm(h, wh) + mm(sb, wa)
        s.u_gate[u][...] = gate.astype(BF)
        hid = swish(gate).astype(BF)
        s.u_hid[u][...] = hid
        y, r = norm_rows(mm(hid, wo))
        s.u_y[u][...] = y.astype(BF)
        s.u_r[u][...] = wide(r)
        return (h.astype(F32) + y).astype(BF)

    def update_back(u, g, wh, wa, wo):
        dz = norm_back(g, s.u_y[u][...].astype(F32), s.u_r[u][:, :1]).astype(BF)
        s.dz[...] = dz
        dgate = (mt(dz, wo) * swish_grad(s.u_gate[u][...].astype(F32))).astype(BF)
        s.dgate[...] = dgate
        return g + mt(dgate, wh), mt(dgate, wa)

    def neighbour(k):
        if k < 2:
            return (lax.rem(w.lat + (ny - 1 if k == 0 else 1), ny), me)
        return (w.lat, lax.rem(me + (n - 1 if k == 2 else 1), n))

    def halo_copy(src, dst, offset, event, k):
        j = OPPOSITE[k]
        return pltpu.make_async_remote_copy(
            src_ref=src.at[pl.ds(k * B, B)],
            dst_ref=dst.at[pl.ds(offset + j * B, B)],
            send_sem=s.halo_ss.at[event * 4 + j],
            recv_sem=s.halo_rs.at[event * 4 + j],
            device_id=neighbour(k),
            device_id_type=MESH,
        )

    s.ext[0][pl.ds(0, T)] = update(
        0, mesh_in[...], s.acc[...], encw[4], encw[5], encw[6]
    )
    proc_copy.wait()
    procw = s.procw
    e_tiles = edges * B // T

    for r in range(ROUNDS):
        ext = s.ext[r]
        latent = ext[pl.ds(0, T)]
        s.hsend[r][...] = mm(s.H[...], latent).astype(BF)
        copies = [halo_copy(s.hsend[r], ext, T, r, k) for k in range(4)]
        for c in copies:
            c.start()
        s.gsum[...] = mm(latent, procw[r, 1]).astype(BF)
        for c in copies:
            c.wait()
        total = jnp.zeros((T, L), F32)
        for t in range(e_tiles):
            at = pl.ds(t * T, T)
            pick = s.Pr[at]
            pre = mm(mm(s.Ps[at], ext[...]).astype(BF), procw[r, 0]) + mm(pick, s.gsum[...])
            s.e_pre[r][at] = pre.astype(BF)
            act = swish(pre).astype(BF)
            s.e_act[r][at] = act
            msg, rstd = norm_rows(mm(act, procw[r, 2]))
            s.e_r[r][at] = wide(rstd)
            msg = msg.astype(BF)
            s.e_msg[r][at] = msg
            total = total + tm(pick, msg)
        new = update(r + 1, latent, total, procw[r, 3], procw[r, 4], procw[r, 5])
        if r + 1 < ROUNDS:
            s.ext[r + 1][pl.ds(0, T)] = new
        else:
            out_lat[...] = new

    parts = []
    for p, count in enumerate((6, 6, 6, 2)):
        refs = Space()
        refs.own, refs.yrecv, refs.zrecv, refs.xrecv = s.own[p], s.yrecv[p], s.zrecv[p], s.xrecv[p]
        refs.fin, refs.swap = s.fin[p], s.swap[p]
        refs.crecv = s.crecv[p % 2].at[:, pl.ds(0, count * per), :]
        parts.append(Scatter(cfg, w, refs, s.rs_ss, s.rs_rs, p * hops, count * per))

    band = L // ny
    band_chips = nz * nx

    def outer_pair(p, pair, first, second):
        own = s.own[p]

        def body(i, _):
            at = pl.ds(pl.multiple_of(i * band, band), band)
            both = []
            for a, b in (first, second):
                both.append(tm(a[:, at], b[...]).reshape(band_chips, per, b.shape[1]))
            own[pl.ds(i * band_chips, band_chips), pl.ds(pair * 2 * per, 2 * per), :] = (
                jnp.concatenate(both, axis=1).astype(BF)
            )
            return 0

        lax.fori_loop(0, ny, body, 0)

    g = mgrad[...].astype(F32)
    for r in reversed(range(ROUNDS)):
        p = ROUNDS - 1 - r
        ext = s.ext[r]
        lat_ref = ext.at[pl.ds(0, T)]
        gh, gs = update_back(r + 1, g, procw[r, 3], procw[r, 4], procw[r, 5])
        s.gh[...] = gh
        s.gsum[...] = gs.astype(BF)
        if p > 0:
            parts[p - 1].start_y()
        for t in range(e_tiles):
            at = pl.ds(t * T, T)
            gmsg = mm(s.Pr[at], s.gsum[...])
            gz = norm_back(gmsg, s.e_msg[r][at].astype(F32), s.e_r[r][at, :1]).astype(BF)
            s.e_msg[r][at] = gz
            dpre = mt(gz, procw[r, 2]) * swish_grad(s.e_pre[r][at].astype(F32))
            s.e_pre[r][at] = dpre.astype(BF)
        dpre = s.e_pre[r][...]
        gext = tm(s.Ps[...], dpre)
        s.bsend[r][...] = gext[T:].astype(BF)
        s.acc[...] = gext[:T]
        copies = [halo_copy(s.bsend[r], s.brecv[r], 0, ROUNDS + r, k) for k in range(4)]
        for c in copies:
            c.start()
        drecv = tm(s.Pr[...], dpre).astype(BF)
        s.drecv[...] = drecv
        s.gh[...] += mt(drecv, procw[r, 1])
        outer_pair(p, 0, (lat_ref, s.drecv), (s.e_act[r], s.e_msg[r]))
        outer_pair(p, 1, (lat_ref, s.dgate), (s.u_s[r + 1], s.dgate))
        for c in copies:
            c.wait()
        dproj = (s.acc[...] + tm(s.H[...], s.brecv[r][...])).astype(BF)
        s.dproj[...] = dproj
        g = s.gh[...] + mt(dproj, procw[r, 0])
        outer_pair(p, 2, (s.u_hid[r + 1], s.dz), (lat_ref, s.dproj))
        parts[p].start_core()

    gh, gs = update_back(0, g, encw[4], encw[5], encw[6])
    s.gh[...] = gh
    s.gsum[...] = gs.astype(BF)
    sent_all(ids_args)
    sent_all(fwd_args)
    s.acc[...] = jnp.zeros((T, L), F32)

    def edge_back(i, _):
        t = lax.rem(me // ppt + i, tiles)
        at = pl.ds(pl.multiple_of(t * T, T), T)
        pick = s.Pm[at]
        gmsg = mm(pick, s.gsum[...])
        gz = norm_back(gmsg, s.g_msg[at].astype(F32), s.g_r[at, :1]).astype(BF)
        s.g_msg[at] = gz
        dpre = (mt(gz, encw[3]) * swish_grad(s.g_pre[at].astype(F32))).astype(BF)
        s.g_pre[at] = dpre
        s.acc[...] += tm(pick, dpre)
        s.sendbuf[at] = mt(dpre, encw[1]).astype(BF)
        for q in range(ppt):
            to = t * ppt + q

            @pl.when(to != me)
            def _():
                row_copy(*back_args, to).start()

        return 0

    lax.fori_loop(0, tiles, edge_back, 0)
    keep_own(back_args)
    parts[1].start_y()
    drecv = s.acc[...].astype(BF)
    s.drecv[...] = drecv
    out_gin[...] = s.gh[...] + mt(drecv, encw[2])
    outer_pair(2, 0, (s.recvbuf, s.g_pre), (s.g_act, s.g_msg))
    outer_pair(2, 1, (mesh_in, s.drecv), (mesh_in, s.dgate))
    outer_pair(2, 2, (s.u_s[0], s.dgate), (s.u_hid[0], s.dz))
    parts[2].start_core()
    parts[0].start_z()
    parts[2].start_y()
    parts[0].start_x()

    s.acc[...] = jnp.zeros((T, L), F32)

    def back_tile(i, _):
        t = lax.rem(me // ppt + tiles - i, tiles)
        for q in range(ppt):
            frm = t * ppt + q

            @pl.when(frm != me)
            def _():
                row_wait(*back_args, frm).wait_recv()

        at = pl.ds(pl.multiple_of(t * T, T), T)
        s.acc[...] += tm(s.G[at], s.backbuf[at])
        return 0

    lax.fori_loop(0, tiles, back_tile, 0)
    dgz = norm_back(s.acc[...], s.grid_norm[...], s.grid_r[:, :1]).astype(BF)
    s.dz[...] = dgz
    dgpre = (mt(dgz, encw[0]) * swish_grad(s.emb_pre[...])).astype(BF)
    s.dgate[...] = dgpre

    def outer_last(i, _):
        own = s.own[3]
        at = pl.ds(pl.multiple_of(i * band, band), band)
        first = tm(s.emb_act[:, at], s.dz[...]).reshape(band_chips, per, L)
        second = tm(s.dgate[:, at], gx[...]).reshape(band_chips, per, HALF)
        second = jnp.concatenate([second, jnp.zeros((band_chips, per, HALF), F32)], axis=2)
        own[pl.ds(i * band_chips, band_chips)] = jnp.concatenate([first, second], axis=1).astype(BF)
        return 0

    lax.fori_loop(0, ny, outer_last, 0)
    parts[3].start_core()
    parts[1].start_z()
    parts[0].start_swap()
    parts[3].start_y()
    parts[2].start_z()
    parts[1].start_x()
    parts[3].start_z()
    parts[2].start_x()
    parts[1].start_swap()
    parts[3].start_x()
    parts[2].start_swap()
    parts[3].start_swap()
    sent_all(back_args)

    left, right = pl.ds(0, HALF), pl.ds(HALF, HALF)
    for p in range(ROUNDS):
        for k, (a, b) in zip((1, 2, 3, 4, 5, 0), parts[p].finish()):
            out_proc[ROUNDS - 1 - p, k, :, left] = a
            out_proc[ROUNDS - 1 - p, k, :, right] = b
    for k, (a, b) in zip((1, 3, 2, 4, 5, 6), parts[2].finish()):
        out_enc[k, :, left] = a
        out_enc[k, :, right] = b
    last = parts[3].finish()
    out_enc[0, :, left], out_enc[0, :, right] = last[0]
    out_emb[...] = last[1][0]


def on_device(
    cfg,
    grid_x,
    mesh_in,
    mesh_grad,
    embed_in,
    enc_weights,
    proc_weights,
    g2m_grid,
    g2m_mesh,
    mesh_send,
    mesh_recv,
    halo_idx,
):
    n = lax.axis_size("lon")
    count = g2m_grid.shape[0]
    cap = (count + n - 1) // n
    variables = grid_x.shape[1]
    chips = cfg[0] * cfg[1] * cfg[2]
    mine = L // chips // 2
    gx = jnp.pad(grid_x, ((0, 0), (0, HALF - variables)))
    emb = jnp.pad(embed_in, ((0, HALF - variables), (0, 0)))
    plan = scratch_plan(cfg, n, n * cap, mesh_send.shape[0])
    vmem = pl.BlockSpec(memory_space=pltpu.VMEM)
    smem = pl.BlockSpec(memory_space=pltpu.SMEM)
    hbm = pl.BlockSpec(memory_space=pl.ANY)
    latent, grad_in, enc, proc, emb_t = pl.pallas_call(
        functools.partial(kernel, cfg, n, cap, plan),
        out_shape=(
            jax.ShapeDtypeStruct((T, L), BF),
            jax.ShapeDtypeStruct((T, L), F32),
            jax.ShapeDtypeStruct((7, mine, L), F32),
            jax.ShapeDtypeStruct((ROUNDS, 6, mine, L), F32),
            jax.ShapeDtypeStruct((mine, HALF), F32),
        ),
        in_specs=[vmem] * 4 + [hbm] * 2 + [vmem] * 3 + [smem] * 3,
        out_specs=(vmem,) * 5,
        scratch_shapes=leaves(plan),
        compiler_params=pltpu.CompilerParams(
            collective_id=0, has_side_effects=True, vmem_limit_bytes=62 * 1024 * 1024
        ),
    )(
        gx,
        mesh_in,
        mesh_grad,
        emb,
        enc_weights,
        proc_weights,
        g2m_mesh.reshape(1, count),
        g2m_mesh.reshape(count, 1),
        g2m_grid.reshape(1, count),
        mesh_send,
        mesh_recv,
        halo_idx.reshape(4),
    )
    return latent, grad_in, enc, proc, emb_t[:, :variables].T


def solution(mesh):
    n = mesh.shape["lon"]
    nx = 4 if n == 32 else 2
    cfg = (mesh.shape["lat"], n // (2 * nx), nx)
    return jax.shard_map(
        functools.partial(on_device, cfg),
        mesh=mesh,
        in_specs=(
            P(("lat", "lon"), None),
            P(("lat", "lon"), None),
            P(("lat", "lon"), None),
            P(),
            P(),
            P(),
            P(("lat", "lon")),
            P(("lat", "lon")),
            P(("lat", "lon")),
            P(("lat", "lon")),
            P(("lat", "lon"), None, None),
        ),
        out_specs=(
            P(("lat", "lon"), None),
            P(("lat", "lon"), None),
            P(None, ("lat", "lon"), None),
            P(None, None, ("lat", "lon"), None),
            P(None, ("lat", "lon")),
        ),
        check_vma=False,
    )
```

time: 541 us -> 179 us (0.33)
  waiting for transfers between devices: 243 us -> 0 us
  Pallas kernels: 0 us -> 165 us
  matrix products: 135 us -> 0 us
  starting transfers between devices: 64.2 us -> 0 us
  other arithmetic: 35.2 us -> 0 us
  between operations: 23.8 us -> 0.65 us
  local copies, waits for them, and re-layouts: 35 us -> 12.5 us
    unnamed x2 -> x0, waiting for transfers between devices: 219 us -> none
    pallas_call x0 -> x1, Pallas kernels: none -> 165 us  [on_device(): pl.pallas_call(functools.partial(kernel, cfg, n, cap, plan), out_shape=(j...]
    dot_general x72 -> x0, matrix products: 135 us -> none  [the longest x22 40.3 us: matmul(): return jnp.dot(first_op, second_op, preferred_element_type=jnp.float32)]
    ppermute x16 -> x0, starting transfers between devices: 38.3 us -> none  [the longest x8 20.2 us: extended(): after = lax.ppermute(leading, axis, down)]
    all_to_all x3 -> x0, starting transfers between devices: 25.6 us -> none  [the longest x1 10.2 us: on_device(): lax.all_to_all(by_transpose(grad_pre_bf, enc_weights[1]).reshape(lon_coun...]
    all_to_all x3 -> x0, waiting for transfers between devices: 24 us -> none  [the longest x1 12 us: on_device(): lax.all_to_all(send_blocks, 'lon', split_axis=0, concat_axis=0, tiled=True)]
    gather x12 -> x0, local copies, waits for them, and re-layouts: 19.5 us -> none  [the longest x4 5.64 us: on_device(): edge_pre = (ext_proj[mesh_send] + recv_side[mesh_recv]).reshape(-1, width)]
    convert_element_type x14 -> x0, other arithmetic: 15 us -> none  [the longest x4 6.71 us: on_device(): edge_act = jax.nn.silu(edge_pre).astype(jnp.bfloat16)]
  transfers between devices with their start and end apart: 20 -> 0, of which waited for: 5 -> 0; matrix products, arithmetic and copies ran while one was open for 9% -> 0% of each run, Pallas kernels for 0% -> 0%
where the time goes in v1:
time: 179 us; the launch traced here: 178 us
  Pallas kernels  165 us (92%)
  local copies, waits for them, and re-layouts  12.5 us (7%)
    pallas_call x1, Pallas kernels, on_device(): pl.pallas_call(functools.partial(kernel, cfg, n, cap, plan), out_shape=(j...  165 us
    unnamed x5, local copies, waits for them, and re-layouts  7.51 us

profile of v1, /device:TPU:1, one launch (start us, length us, event | category | flops | bytes accessed | tf_op | source)
XLA Modules:
  0.0 178.3 jit_solution(5250540345795339695)
XLA Ops:
  0.6 1.3 copy.17.mcol
  2.0 1.0 copy.16
  3.0 0.7 pad.8.gx
  3.7 1.7 pad.9.emb
  5.3 165.2 %shard_map.146 = (bf16[256,512]{1,0:T(8,128)(2,1)}, f32[256,512]{1,0:T(8,128)}, f32[7,4,512]{2,1,0:T(4,128)}, f32[2,6,4,512]{3,2,1,0:T(4,128)}, f32[4,256]{1,0:T(4,128)}) custom-call(bf16[256,256]{1,0:T(8,128)(2,1)} %pad.8.gx, bf16[256,512]{1,0:T(8,128)(2,1)} %mesh_in.1, bf16[256,512]{1,0:T(8,128)(2,1)} %mgrad.1, bf16[256,512]{1,0:T(8,128)(2,1)} %pad.9.emb, ...), custom_call_target="tpu_custom_call" | custom-call | tf_op jit(solution)/shard_map/pallas_call | solution.py:789
  170.5 1.3 slice_bitcast_fusion
  171.8 1.7 copy.22
  173.5 1.9 %copy.23 = f32[256,512]{1,0:T(8,128)} copy(f32[256,512]{1,0:T(8,128)} %get-tuple-element.21) | data formatting | bytes 1048576
  175.3 1.4 copy.24
  176.8 1.5 copy.25

commit v2 on v1

v2 whole, which is shorter than its diff:
```python
import functools

import jax
import jax.numpy as jnp
from jax import lax
from jax.experimental import pallas as pl
from jax.experimental.pallas import tpu as pltpu
from jax.sharding import PartitionSpec as P

B = 32
L = 512
T = 256
MB = 8
ROUNDS = 2
EPSILON = 1e-05
BF = jnp.bfloat16
F32 = jnp.float32
MESH = pl.DeviceIdType.MESH
HALF = L // 2
OPPOSITE = (1, 0, 3, 2)
STRIDE = 19


def mm(a, b):
    return jnp.dot(a, b, preferred_element_type=F32)


def mt(a, b):
    return lax.dot_general(a, b, (((1,), (1,)), ((), ())), preferred_element_type=F32)


def tm(a, b):
    return lax.dot_general(a, b, (((0,), (0,)), ((), ())), preferred_element_type=F32)


def sigmoid(x):
    return 0.5 * jnp.tanh(0.5 * x) + 0.5


def swish(x):
    return x * sigmoid(x)


def swish_grad(x):
    s = sigmoid(x)
    return s * (1.0 + x * (1.0 - s))


def norm_rows(z):
    centred = z - jnp.mean(z, axis=-1, keepdims=True)
    r = lax.rsqrt(jnp.mean(centred * centred, axis=-1, keepdims=True) + EPSILON)
    return centred * r, r


def norm_back(g, y, r):
    return r * (
        g - jnp.mean(g, axis=-1, keepdims=True) - y * jnp.mean(g * y, axis=-1, keepdims=True)
    )


def iota(shape, dim):
    return lax.broadcasted_iota(jnp.int32, shape, dim)


def wide(r):
    return jnp.broadcast_to(r, (r.shape[0], 128))


class Group:
    def __init__(self, cfg, w, refs, sems, base, rows):
        self.cfg, self.w, self.refs, self.rows = cfg, w, refs, rows
        self.send, self.recv = sems
        self.base = base
        self.lanes = []

    def copy(self, src, dst, index, device):
        c = pltpu.make_async_remote_copy(
            src_ref=src,
            dst_ref=dst,
            send_sem=self.send.at[index],
            recv_sem=self.recv.at[index],
            device_id=device,
            device_id_type=MESH,
        )
        c.start()
        return c

    def half(self, which):
        return pl.ds(pl.multiple_of(which * HALF, HALF), HALF)

    def start_core(self):
        w = self.w
        src = self.refs.own.at[:, :, :, :, self.half(1 - w.core)]
        self.core = self.copy(src, self.refs.crecv, self.base, (w.lat, w.sibling))

    def add_core(self):
        own, crecv = self.refs.own, self.refs.crecv
        mine = self.half(self.w.core)
        ny, nz, _ = self.cfg
        self.core.wait()

        def body(y, _):
            for z in range(nz):
                total = own[y, z, :, :, mine].astype(F32) + crecv[y, z].astype(F32)
                own[y, z, :, :, mine] = total.astype(BF)
            return 0

        lax.fori_loop(0, ny, body, 0)

    def step(self):
        for lane in self.lanes:
            lane.step()

    def start_swap(self):
        w = self.w
        self.step()
        self.swapped = self.copy(
            self.refs.fin, self.refs.swap, self.base + 1, (w.lat, w.sibling)
        )

    def finish(self):
        w, (ny, nz, nx) = self.w, self.cfg
        self.swapped.wait()
        per = L // (ny * nz * nx)
        mine, other = self.refs.fin[...], self.refs.swap[...]
        left = jnp.where(w.core == 0, mine, other)
        right = jnp.where(w.core == 0, other, mine)
        keep = []
        for k in range(self.rows // per):
            pair = []
            for side in (left, right):
                rows = side[k * per : (k + 1) * per]
                pair.append(jnp.where(w.core == 0, rows[: per // 2], rows[per // 2 :]))
            keep.append(pair)
        return keep


class Lane:
    def __init__(self, group, recvs, base, rows, cols, order):
        self.group, self.recvs, self.base = group, recvs, base
        self.rows, self.cols, self.order = rows, cols, order
        w = group.w
        self.at = (w.lat, w.z, w.x)
        self.fixed = [slice(None)] * 3
        self.stage = 0
        self.flying = []

    def index(self, fixed):
        start = pl.multiple_of(self.group.w.core * HALF + self.cols[0], 128)
        return tuple(fixed) + (pl.ds(*self.rows), pl.ds(start, self.cols[1]))

    def device(self, axis, to):
        y, z, x = [to if a == axis else c for a, c in enumerate(self.at)]
        return (y, (z * self.group.cfg[2] + x) * 2 + self.group.w.core)

    def step(self):
        if self.stage > 0:
            self.collect()
        if self.stage < 3:
            self.launch()
        self.stage += 1

    def launch(self):
        axis, own = self.order[self.stage], self.group.refs.own
        size = self.group.cfg[axis]
        for j in range(1, size):
            to = lax.rem(self.at[axis] + j, size)
            there = list(self.fixed)
            there[axis] = to
            self.flying.append(
                self.group.copy(
                    own.at[self.index(there)],
                    self.recvs[self.stage].at[j - 1],
                    self.base,
                    self.device(axis, to),
                )
            )
            self.base += 1
        self.fixed[axis] = self.at[axis]

    def collect(self):
        own, recv = self.group.refs.own, self.recvs[self.stage - 1]
        for c in self.flying:
            c.wait()
        self.flying = []
        peers = recv.shape[0]
        free = [a for a in range(3) if isinstance(self.fixed[a], slice)]
        if not free:
            total = own[self.index(self.fixed)].astype(F32)
            for j in range(peers):
                total = total + recv[j].astype(F32)
            self.group.refs.fin[pl.ds(*self.rows), pl.ds(*self.cols)] = total
            return
        for i in range(self.group.cfg[free[0]]):
            here = list(self.fixed)
            here[free[0]] = i
            total = own[self.index(here)].astype(F32)
            for j in range(peers):
                total = total + recv[j, i].astype(F32)
            own[self.index(here)] = total.astype(BF)


class Space:
    pass


Y, Z, X = 0, 1, 2
GROUPS = (
    (6, ((0, 1, 0, HALF, (Y, Z, X)), (1, 1, 0, HALF, (Z, X, Y)), (2, 1, 0, HALF, (X, Y, Z)))),
    (6, ((0, 3, 0, HALF, (Y, Z, X)),)),
    (6, ((0, 1, 0, HALF, (Y, Z, X)), (1, 1, 0, HALF, (Z, X, Y)), (2, 1, 0, HALF, (X, Y, Z)))),
    (2, ((0, 1, 0, 128, (Y, Z, X)), (0, 1, 128, 128, (Z, X, Y)))),
)


def scratch_plan(cfg, n, slots, edges):
    ny, nz, nx = cfg
    per = L // (ny * nz * nx)
    rows = slots * B
    ids = slots * 8
    v = Space()

    def vm(*shape, dtype=BF):
        return pltpu.VMEM(shape, dtype)

    v.encw = vm(7, L, L)
    v.procw = vm(ROUNDS, 6, L, L)
    v.gxp = vm(HALF, T)
    v.emb_pre = vm(T, L)
    v.emb_act = vm(T, L)
    v.grid_norm = vm(T, L)
    v.grid_r = vm(T, 128, dtype=F32)
    v.G = vm(rows, T)
    v.sendbuf = vm(rows, L)
    v.recvbuf = vm(rows, L)
    v.backbuf = vm(rows, L)
    v.ids_send = vm(ids, 128)
    v.ids_recv = vm(ids, 128)
    v.Pm = vm(rows, T)
    v.recv_proj = vm(T, L)
    v.g_pre = vm(rows, L)
    v.g_act = vm(rows, L)
    v.g_msg = vm(rows, L)
    v.g_r = vm(rows, 128)
    v.acc = vm(T, L, dtype=F32)
    v.gsum = vm(T, L)
    v.u_s, v.u_gate, v.u_hid, v.u_y, v.u_r = [], [], [], [], []
    for u in range(ROUNDS + 1):
        v.u_s.append(vm(T, L))
        v.u_gate.append(vm(T, L))
        v.u_hid.append(vm(T, L))
        v.u_y.append(vm(T, L))
        v.u_r.append(vm(T, 128, dtype=F32))
    v.dz = vm(T, L)
    v.dgate = vm(T, L)
    v.drecv = vm(T, L)
    v.Pc = vm(edges * B, 2 * T)
    v.Ph = vm(edges * B, 4 * B)
    v.H = vm(4 * B, T)
    v.lat, v.halo, v.hsend, v.bsend, v.brecv = [], [], [], [], []
    v.e_pre, v.e_act, v.e_msg, v.e_r = [], [], [], []
    for r in range(ROUNDS):
        v.lat.append(vm(T, L))
        v.halo.append(vm(4 * B, L))
        v.hsend.append(vm(4 * B, L))
        v.bsend.append(vm(4 * B, L))
        v.brecv.append(vm(4 * B, L))
        v.e_pre.append(vm(edges * B, L))
        v.e_act.append(vm(edges * B, L))
        v.e_msg.append(vm(edges * B, L))
        v.e_r.append(vm(edges * B, 128, dtype=F32))
    v.own, v.crecv, v.fin, v.swap, v.lanes = [], [], [], [], []
    sems = 0
    for p, (count, lanes) in enumerate(GROUPS):
        r = count * per
        v.own.append(vm(*cfg, r, L))
        if p < 2:
            v.crecv.append(vm(*cfg, r, HALF))
        v.fin.append(vm(r, HALF, dtype=F32))
        v.swap.append(vm(r, HALF, dtype=F32))
        sems += 2
        for _, some, _, width, order in lanes:
            left = [0, 1, 2]
            for axis in order:
                left.remove(axis)
                free = [cfg[a] for a in left]
                v.lanes.append(vm(cfg[axis] - 1, *free, some * 2 * per, width))
                sems += cfg[axis] - 1
    dma = pltpu.SemaphoreType.DMA
    v.w_sem = dma((2,))
    v.ids_ss, v.ids_rs = dma((n,)), dma((n,))
    v.fwd_ss, v.fwd_rs = dma((n,)), dma((n,))
    v.back_ss, v.back_rs = dma((n,)), dma((n,))
    v.halo_ss, v.halo_rs = dma((8 * ROUNDS,)), dma((8 * ROUNDS,))
    v.rs_ss, v.rs_rs = dma((sems,)), dma((sems,))
    return v


def leaves(plan):
    return [x for v in vars(plan).values() for x in (v if isinstance(v, list) else [v])]


def bind(plan, refs):
    rest, out = iter(refs), Space()
    for name, v in vars(plan).items():
        setattr(out, name, [next(rest) for _ in v] if isinstance(v, list) else next(rest))
    return out


def kernel(
    cfg,
    n,
    cap,
    plan,
    gxt,
    mesh_in,
    mgrad,
    emb,
    encw_hbm,
    procw_hbm,
    mrow,
    grow,
    msend,
    mrecv,
    hidx,
    out_lat,
    out_gin,
    out_enc,
    out_proc,
    out_emb,
    *scratch,
):
    s = bind(plan, scratch)
    ny, nz, nx = cfg
    per = L // (ny * nz * nx)
    slots = n * cap
    tiles = slots * B // T
    ppt = T // (cap * B)
    edges = msend.shape[0]
    variables = gxt.shape[0]

    w = Space()
    w.lat, w.lon = lax.axis_index("lat"), lax.axis_index("lon")
    w.core = lax.rem(w.lon, 2)
    w.sibling = w.lon + 1 - 2 * w.core
    w.x = lax.rem(w.lon // 2, nx)
    w.z = w.lon // (2 * nx)
    me = w.lon

    enc_copy = pltpu.make_async_copy(encw_hbm, s.encw, s.w_sem.at[0])
    proc_copy = pltpu.make_async_copy(procw_hbm, s.procw, s.w_sem.at[1])
    enc_copy.start()
    proc_copy.start()

    barrier = pltpu.get_barrier_semaphore()

    def greet(k, _):
        pl.semaphore_signal(
            barrier, inc=1, device_id=(w.lat, lax.rem(me + k, n)), device_id_type=MESH
        )
        return 0

    lax.fori_loop(1, n, greet, 0)
    for j in range(1, ny):
        pl.semaphore_signal(
            barrier, inc=1, device_id=(lax.rem(w.lat + j, ny), me), device_id_type=MESH
        )

    count = mrow.shape[1]
    owner = (mrow[...] >> 3) & (n - 1)
    owner_hot = jnp.where(iota((n, count), 0) == owner, 1.0, 0.0)
    same = tm(owner_hot.astype(BF), owner_hot.astype(BF))
    before = iota((count, count), 0) < iota((count, count), 1)
    rank = jnp.sum(jnp.where(before, same, 0.0), axis=0, keepdims=True)
    far_z = (owner // (2 * nx) + nz - w.z) & (nz - 1)
    far_x = ((owner // 2) & (nx - 1)) + nx - w.x & (nx - 1)
    far = (far_z * nx + far_x) * 2 + ((owner + w.core) & 1)
    place_of = (far * pow(STRIDE, -1, n) + n - 1) & (n - 1)
    slot = place_of.astype(F32) * cap + rank
    hot = iota((slots, count), 0).astype(F32) == slot
    block = jnp.sum(jnp.where(hot, grow[...].astype(F32) + 1.0, 0.0), axis=1, keepdims=True) - 1.0
    dest = (
        jnp.sum(jnp.where(hot, (mrow[...] & (MB - 1)).astype(F32) + 1.0, 0.0), axis=1, keepdims=True)
        - 1.0
    )
    spread = (iota((slots * 8, slots), 0) >> 3) == iota((slots * 8, slots), 1)
    s.ids_send[...] = mm(
        jnp.where(spread, 1.0, 0.0).astype(BF),
        jnp.broadcast_to(dest, (slots, 128)).astype(BF),
    ).astype(BF)

    def at_offset(p, sign):
        q = lax.rem(STRIDE * (p + 1), n)
        z = lax.rem(w.z + nz + sign * (q // (2 * nx)), nz)
        x = lax.rem(w.x + nx + sign * lax.rem(q // 2, nx), nx)
        return (z * nx + x) * 2 + lax.rem(w.core + lax.rem(q, 2), 2)

    def row_copy(src, dst, size, ss, rs, sign, p):
        at = pl.ds(pl.multiple_of(p * size, size), size)
        return pltpu.make_async_remote_copy(
            src_ref=src.at[at],
            dst_ref=dst.at[at],
            send_sem=ss.at[p],
            recv_sem=rs.at[p],
            device_id=(w.lat, at_offset(p, sign)),
            device_id_type=MESH,
        )

    ids_args = (s.ids_send, s.ids_recv, cap * 8, s.ids_ss, s.ids_rs, 1)
    fwd_args = (s.sendbuf, s.recvbuf, cap * B, s.fwd_ss, s.fwd_rs, 1)
    back_args = (s.sendbuf, s.backbuf, cap * B, s.back_ss, s.back_rs, -1)

    def send_all(args):
        def body(p, _):
            row_copy(*args, p).start()
            return 0

        lax.fori_loop(0, n - 1, body, 0)

    def sent_all(args):
        def body(p, _):
            row_copy(*args, p).wait_send()
            return 0

        lax.fori_loop(0, n - 1, body, 0)

    def keep_own(args):
        src, dst, size = args[:3]
        at = pl.ds((n - 1) * size, size)
        dst[at] = src[at]

    s.gxp[...] = jnp.zeros((HALF, T), BF)
    s.gxp[pl.ds(0, variables), :] = gxt[...]
    embp = s.sendbuf.at[pl.ds(0, HALF)]
    embp[...] = jnp.zeros((HALF, L), BF)
    embp[pl.ds(0, variables), :] = emb[...]
    emb_pre = tm(s.gxp[...], embp[...])
    s.emb_pre[...] = emb_pre.astype(BF)
    emb_act = swish(emb_pre).astype(BF)
    s.emb_act[...] = emb_act
    enc_copy.wait()
    encw = s.encw
    grid_norm, grid_r = norm_rows(mm(emb_act, encw[0]))
    s.grid_norm[...] = grid_norm.astype(BF)
    s.grid_r[...] = wide(grid_r)

    pl.semaphore_wait(barrier, n - 1 + ny - 1)
    send_all(ids_args)

    col = iota((T, T), 1)
    diag = (col & (B - 1)) == (iota((T, T), 0) & (B - 1))
    col_block = (col >> 5).astype(F32)
    block_b = jnp.broadcast_to(block, (slots, T)).astype(BF)

    def fill(t, _):
        at = pl.ds(pl.multiple_of(t * T, T), T)
        expand = ((iota((T, slots), 0) + t * T) >> 5) == iota((T, slots), 1)
        value = mm(jnp.where(expand, 1.0, 0.0).astype(BF), block_b)
        pick = jnp.where(diag & (value == col_block), 1.0, 0.0).astype(BF)
        s.G[at] = pick
        s.sendbuf[at] = mm(pick, s.grid_norm[...]).astype(BF)
        for q in range(ppt):
            p = t * ppt + q

            @pl.when(p < n - 1)
            def _():
                row_copy(*fwd_args, p).start()

        return 0

    lax.fori_loop(0, tiles, fill, 0)
    keep_own(ids_args)
    keep_own(fwd_args)

    s.recv_proj[...] = mm(mesh_in[...], encw[2]).astype(BF)

    def place(columns):
        col = iota((B, columns), 1)
        return (col & (B - 1)) == iota((B, columns), 0), col >> 5

    diag_c, block_c = place(2 * T)
    diag_h, block_h = place(4 * B)
    diag_l, block_l = place(T)
    for e in range(edges):
        sender = msend[e]
        local = jnp.where(sender < MB, sender, -1)
        hit = (block_c == local) | (block_c == mrecv[e] + MB)
        s.Pc[pl.ds(e * B, B)] = jnp.where(diag_c & hit, 1.0, 0.0).astype(BF)
        s.Ph[pl.ds(e * B, B)] = jnp.where(diag_h & (block_h == sender - MB), 1.0, 0.0).astype(BF)
    for k in range(4):
        s.H[pl.ds(k * B, B)] = jnp.where(diag_l & (block_l == hidx[k]), 1.0, 0.0).astype(BF)

    def ids_wait(p, _):
        row_copy(*ids_args, p).wait_recv()
        return 0

    lax.fori_loop(0, n - 1, ids_wait, 0)
    id_rows = ppt * cap * 8
    id_pick = iota((T, id_rows), 1) == ((iota((T, id_rows), 0) >> 5) << 3)
    id_pick = jnp.where(id_pick, 1.0, 0.0).astype(BF)

    def pick_mesh(t, _):
        value = mm(id_pick, s.ids_recv[pl.ds(pl.multiple_of(t * id_rows, id_rows), id_rows)])
        value = jnp.concatenate([value, value], axis=1)
        s.Pm[pl.ds(pl.multiple_of(t * T, T), T)] = jnp.where(
            diag & (value == col_block), 1.0, 0.0
        ).astype(BF)
        return 0

    lax.fori_loop(0, tiles, pick_mesh, 0)
    s.acc[...] = jnp.zeros((T, L), F32)

    def edge_tile(t, _):
        for q in range(ppt):
            p = t * ppt + q

            @pl.when(p < n - 1)
            def _():
                row_copy(*fwd_args, p).wait_recv()

        at = pl.ds(pl.multiple_of(t * T, T), T)
        pick = s.Pm[at]
        pre = mm(s.recvbuf[at], encw[1]) + mm(pick, s.recv_proj[...])
        s.g_pre[at] = pre.astype(BF)
        act = swish(pre).astype(BF)
        s.g_act[at] = act
        msg, r = norm_rows(mm(act, encw[3]))
        s.g_r[at] = wide(r).astype(BF)
        msg = msg.astype(BF)
        s.g_msg[at] = msg
        s.acc[...] += tm(pick, msg)
        return 0

    lax.fori_loop(0, tiles, edge_tile, 0)

    def update(u, h, total, wh, wa, wo):
        sb = total.astype(BF)
        s.u_s[u][...] = sb
        gate = mm(h, wh) + mm(sb, wa)
        s.u_gate[u][...] = gate.astype(BF)
        hid = swish(gate).astype(BF)
        s.u_hid[u][...] = hid
        y, r = norm_rows(mm(hid, wo))
        s.u_y[u][...] = y.astype(BF)
        s.u_r[u][...] = wide(r)
        return (h.astype(F32) + y).astype(BF)

    def update_back(u, wh, wa, wo):
        dz = norm_back(out_gin[...], s.u_y[u][...].astype(F32), s.u_r[u][:, :1]).astype(BF)
        s.dz[...] = dz
        dgate = (mt(dz, wo) * swish_grad(s.u_gate[u][...].astype(F32))).astype(BF)
        s.dgate[...] = dgate
        out_gin[...] += mt(dgate, wh)
        return mt(dgate, wa)

    def neighbour(k):
        if k < 2:
            return (lax.rem(w.lat + (ny - 1 if k == 0 else 1), ny), me)
        return (w.lat, lax.rem(me + (n - 1 if k == 2 else 1), n))

    def halo_copy(src, dst, event, k):
        j = OPPOSITE[k]
        return pltpu.make_async_remote_copy(
            src_ref=src.at[pl.ds(k * B, B)],
            dst_ref=dst.at[pl.ds(j * B, B)],
            send_sem=s.halo_ss.at[event * 4 + j],
            recv_sem=s.halo_rs.at[event * 4 + j],
            device_id=neighbour(k),
            device_id_type=MESH,
        )

    s.lat[0][...] = update(0, mesh_in[...], s.acc[...], encw[4], encw[5], encw[6])
    proc_copy.wait()
    procw = s.procw
    top, bottom = pl.ds(0, T), pl.ds(T, T)
    sent_all(ids_args)
    sent_all(fwd_args)
    proj = s.sendbuf.at[pl.ds(0, 2 * T)]
    mixed = s.sendbuf.at[pl.ds(4 * T, 2 * T)]

    for r in range(ROUNDS):
        latent = s.lat[r][...]
        s.hsend[r][...] = mm(s.H[...], latent).astype(BF)
        copies = [halo_copy(s.hsend[r], s.halo[r], r, k) for k in range(4)]
        for c in copies:
            c.start()
        proj[top] = mm(latent, procw[r, 0]).astype(BF)
        proj[bottom] = mm(latent, procw[r, 1]).astype(BF)
        mixed[...] = mm(s.Pc[...], proj[...]).astype(BF)
        for c in copies:
            c.wait()
        shown = mm(s.halo[r][...], procw[r, 0]).astype(BF)
        pre = mixed[...].astype(F32) + mm(s.Ph[...], shown)
        s.e_pre[r][...] = pre.astype(BF)
        act = swish(pre).astype(BF)
        s.e_act[r][...] = act
        msg, rstd = norm_rows(mm(act, procw[r, 2]))
        s.e_r[r][...] = wide(rstd)
        msg = msg.astype(BF)
        s.e_msg[r][...] = msg
        total = tm(s.Pc[:, bottom], msg)
        new = update(r + 1, latent, total, procw[r, 3], procw[r, 4], procw[r, 5])
        if r + 1 < ROUNDS:
            s.lat[r + 1][...] = new
        else:
            out_lat[...] = new

    dproj_ref = s.sendbuf.at[pl.ds(2 * T, T)]
    groups = []
    sem = lane_at = 0
    for p, (count, lanes) in enumerate(GROUPS):
        refs = Space()
        refs.own, refs.fin, refs.swap = s.own[p], s.fin[p], s.swap[p]
        refs.crecv = s.crecv[p % 2].at[:, :, :, pl.ds(0, count * per), :]
        group = Group(cfg, w, refs, (s.rs_ss, s.rs_rs), sem, count * per)
        sem += 2
        for first, some, left, width, order in lanes:
            rows = (first * 2 * per, some * 2 * per)
            recvs = s.lanes[lane_at : lane_at + 3]
            group.lanes.append(Lane(group, recvs, sem, rows, (left, width), order))
            lane_at += 3
            sem += ny + nz + nx - 3
        groups.append(group)

    def outer_pair(p, pair, first, second):
        band = L // ny
        for y in range(ny):
            at = pl.ds(y * band, band)
            both = [tm(a[:, at], b[...]).reshape(nz, nx, per, L) for a, b in (first, second)]
            rows = pl.ds(pair * 2 * per, 2 * per)
            s.own[p][y, :, :, rows, :] = jnp.concatenate(both, axis=2).astype(BF)

    out_gin[...] = mgrad[...].astype(F32)
    for r in reversed(range(ROUNDS)):
        p = ROUNDS - 1 - r
        gs = update_back(r + 1, procw[r, 3], procw[r, 4], procw[r, 5])
        gmsg = mm(s.Pc[:, bottom], gs.astype(BF))
        gz = norm_back(gmsg, s.e_msg[r][...].astype(F32), s.e_r[r][:, :1]).astype(BF)
        s.e_msg[r][...] = gz
        dpre = (mt(gz, procw[r, 2]) * swish_grad(s.e_pre[r][...].astype(F32))).astype(BF)
        s.e_pre[r][...] = dpre
        s.bsend[r][...] = tm(s.Ph[...], dpre).astype(BF)
        copies = [halo_copy(s.bsend[r], s.brecv[r], ROUNDS + r, k) for k in range(4)]
        for c in copies:
            c.start()
        mixed[...] = tm(s.Pc[...], s.e_pre[r][...]).astype(BF)
        drecv = mixed[bottom]
        s.drecv[...] = drecv
        out_gin[...] += mt(drecv, procw[r, 1])
        outer_pair(p, 0, (s.lat[r], s.drecv), (s.e_act[r], s.e_msg[r]))
        outer_pair(p, 1, (s.lat[r], s.dgate), (s.u_s[r + 1], s.dgate))
        if p > 0:
            groups[p - 1].add_core()
            groups[p - 1].step()
        for c in copies:
            c.wait()
        dproj = (mixed[top].astype(F32) + tm(s.H[...], s.brecv[r][...])).astype(BF)
        dproj_ref[...] = dproj
        out_gin[...] += mt(dproj, procw[r, 0])
        outer_pair(p, 2, (s.u_hid[r + 1], s.dz), (s.lat[r], dproj_ref))
        groups[p].start_core()

    gs = update_back(0, encw[4], encw[5], encw[6])
    s.gsum[...] = gs.astype(BF)
    s.acc[...] = jnp.zeros((T, L), F32)

    def edge_back(t, _):
        at = pl.ds(pl.multiple_of(t * T, T), T)
        pick = s.Pm[at]
        gmsg = mm(pick, s.gsum[...])
        gz = norm_back(gmsg, s.g_msg[at].astype(F32), s.g_r[at, :1].astype(F32)).astype(BF)
        s.g_msg[at] = gz
        dpre = (mt(gz, encw[3]) * swish_grad(s.g_pre[at].astype(F32))).astype(BF)
        s.g_pre[at] = dpre
        s.acc[...] += tm(pick, dpre)
        s.sendbuf[at] = mt(dpre, encw[1]).astype(BF)
        for q in range(ppt):
            p = t * ppt + q

            @pl.when(p < n - 1)
            def _():
                row_copy(*back_args, p).start()

        return 0

    lax.fori_loop(0, tiles // 2, edge_back, 0)
    groups[1].add_core()
    groups[1].step()
    lax.fori_loop(tiles // 2, tiles, edge_back, 0)
    keep_own(back_args)
    groups[0].step()
    drecv = s.acc[...].astype(BF)
    s.drecv[...] = drecv
    out_gin[...] += mt(drecv, encw[2])
    outer_pair(2, 0, (s.recvbuf, s.g_pre), (s.g_act, s.g_msg))
    outer_pair(2, 1, (mesh_in, s.drecv), (mesh_in, s.dgate))
    outer_pair(2, 2, (s.u_s[0], s.dgate), (s.u_hid[0], s.dz))
    groups[2].start_core()
    groups[0].step()

    s.acc[...] = jnp.zeros((T, L), F32)

    def back_tile(t, _):
        for q in range(ppt):
            p = t * ppt + q

            @pl.when(p < n - 1)
            def _():
                row_copy(*back_args, p).wait_recv()

        at = pl.ds(pl.multiple_of(t * T, T), T)
        s.acc[...] += tm(s.G[at], s.backbuf[at])
        return 0

    lax.fori_loop(0, tiles // 2, back_tile, 0)
    groups[2].add_core()
    groups[1].step()
    lax.fori_loop(tiles // 2, tiles, back_tile, 0)
    groups[2].step()
    dgz = norm_back(s.acc[...], s.grid_norm[...].astype(F32), s.grid_r[:, :1]).astype(BF)
    dgpre = (mt(dgz, encw[0]) * swish_grad(s.emb_pre[...].astype(F32))).astype(BF)
    first = tm(s.emb_act[...], dgz).reshape(ny, nz, nx, per, L)
    second = mm(s.gxp[...], dgpre).T.reshape(ny, nz, nx, per, HALF)
    second = jnp.concatenate([second, jnp.zeros_like(second)], axis=4)
    s.own[3][...] = jnp.concatenate([first, second], axis=3).astype(BF)
    groups[3].start_core()
    groups[0].start_swap()
    groups[1].step()
    groups[3].add_core()
    groups[3].step()
    groups[2].step()
    groups[1].start_swap()
    groups[3].step()
    groups[2].step()
    groups[3].step()
    groups[2].start_swap()
    groups[3].start_swap()
    sent_all(back_args)

    left, right = pl.ds(0, HALF), pl.ds(HALF, HALF)
    for p in range(ROUNDS):
        for k, (a, b) in zip((1, 2, 3, 4, 5, 0), groups[p].finish()):
            out_proc[ROUNDS - 1 - p, k, :, left] = a
            out_proc[ROUNDS - 1 - p, k, :, right] = b
    for k, (a, b) in zip((1, 3, 2, 4, 5, 6), groups[2].finish()):
        out_enc[k, :, left] = a
        out_enc[k, :, right] = b
    last = groups[3].finish()
    out_enc[0, :, left], out_enc[0, :, right] = last[0]
    out_emb[...] = last[1][0][:, :variables]


def hand_over(*refs):
    count = len(refs) // 2
    for k in range(count):
        refs[count + k][...] = refs[k][...]


def on_device(
    cfg,
    grid_x,
    mesh_in,
    mesh_grad,
    embed_in,
    enc_weights,
    proc_weights,
    g2m_grid,
    g2m_mesh,
    mesh_send,
    mesh_recv,
    halo_idx,
):
    n = lax.axis_size("lon")
    count = g2m_grid.shape[0]
    cap = (count + n - 1) // n
    variables = grid_x.shape[1]
    mine = L // (cfg[0] * cfg[1] * cfg[2]) // 2
    plan = scratch_plan(cfg, n, n * cap, mesh_send.shape[0])
    vmem = pl.BlockSpec(memory_space=pltpu.VMEM)
    smem = pl.BlockSpec(memory_space=pltpu.SMEM)
    hbm = pl.BlockSpec(memory_space=pl.ANY)
    shapes = (
        jax.ShapeDtypeStruct((T, L), BF),
        jax.ShapeDtypeStruct((T, L), F32),
        jax.ShapeDtypeStruct((7, mine, L), F32),
        jax.ShapeDtypeStruct((ROUNDS, 6, mine, L), F32),
        jax.ShapeDtypeStruct((mine, variables), F32),
    )
    results = pl.pallas_call(
        functools.partial(kernel, cfg, n, cap, plan),
        out_shape=shapes,
        in_specs=[vmem] * 4 + [hbm] * 2 + [vmem] * 2 + [smem] * 3,
        out_specs=(vmem,) * 5,
        scratch_shapes=leaves(plan),
        compiler_params=pltpu.CompilerParams(
            collective_id=0, has_side_effects=True, vmem_limit_bytes=63 * 1024 * 1024
        ),
    )(
        grid_x.T,
        mesh_in,
        mesh_grad,
        embed_in,
        enc_weights,
        proc_weights,
        g2m_mesh.reshape(1, count),
        g2m_grid.reshape(1, count),
        mesh_send,
        mesh_recv,
        halo_idx.reshape(4),
    )
    latent, grad_in, enc, proc, emb_t = pl.pallas_call(
        hand_over,
        out_shape=shapes,
        in_specs=[vmem] * 5,
        out_specs=(vmem,) * 5,
    )(*results)
    return latent, grad_in, enc, proc, emb_t.T


def solution(mesh):
    n = mesh.shape["lon"]
    nx = 4 if n == 32 else 2
    cfg = (mesh.shape["lat"], n // (2 * nx), nx)
    return jax.shard_map(
        functools.partial(on_device, cfg),
        mesh=mesh,
        in_specs=(
            P(("lat", "lon"), None),
            P(("lat", "lon"), None),
            P(("lat", "lon"), None),
            P(),
            P(),
            P(),
            P(("lat", "lon")),
            P(("lat", "lon")),
            P(("lat", "lon")),
            P(("lat", "lon")),
            P(("lat", "lon"), None, None),
        ),
        out_specs=(
            P(("lat", "lon"), None),
            P(("lat", "lon"), None),
            P(None, ("lat", "lon"), None),
            P(None, None, ("lat", "lon"), None),
            P(None, ("lat", "lon")),
        ),
        check_vma=False,
    )
```

time: 179 us -> 133 us (0.74)
  Pallas kernels: 165 us -> 132 us
  local copies, waits for them, and re-layouts: 12.5 us -> 0 us
    pallas_call x1 -> x2, Pallas kernels: 165 us -> 132 us  [the longest x1 130 us: on_device(): pl.pallas_call(functools.partial(kernel, cfg, n, cap, plan), out_shape=sh...]
    unnamed x5 -> x0, local copies, waits for them, and re-layouts: 7.51 us -> none
    pad x2 -> x0, local copies, waits for them, and re-layouts: 2.34 us -> none  [the longest x1 1.66 us: on_device(): emb = jnp.pad(embed_in, ((0, HALF - variables), (0, 0)))]
where the time goes in v2:
time: 133 us
  Pallas kernels  132 us (99%)
    pallas_call x1, Pallas kernels, on_device(): pl.pallas_call(functools.partial(kernel, cfg, n, cap, plan), out_shape=sh...  130 us

profile of v2, /device:TPU:1, one launch (start us, length us, event | category | flops | bytes accessed | tf_op | source)
XLA Modules:
  0.0 133.1 jit_solution(2568197028616738300)
XLA Ops:
  0.6 130.3 %shard_map.146 = (bf16[256,512]{1,0:T(8,128)(2,1)}, f32[256,512]{1,0:T(8,128)}, f32[7,4,512]{2,1,0:T(4,128)}, f32[2,6,4,512]{3,2,1,0:T(4,128)}, f32[4,227]{1,0:T(4,128)}) custom-call(bf16[227,256]{1,0:T(8,128)(2,1)} %bitcast.5, bf16[256,512]{1,0:T(8,128)(2,1)} %mesh_in.1, bf16[256,512]{1,0:T(8,128)(2,1)} %mgrad.1, bf16[227,512]{1,0:T(8,128)(2,1)} %emb.1, ...), custom_call_target="tpu_custom_call" | custom-call | tf_op jit(solution)/shard_map/pallas_call | solution.py:789
  131.0 2.1 %shard_map.147 = (bf16[256,512]{1,0:T(8,128)(2,1)}, f32[256,512]{1,0:T(8,128)}, f32[7,4,512]{2,1,0:T(4,128)}, f32[2,6,4,512]{3,2,1,0:T(4,128)}, f32[4,227]{1,0:T(4,128)}) custom-call(bf16[256,512]{1,0:T(8,128)(2,1)} %get-tuple-element.15.refs_0_, f32[256,512]{1,0:T(8,128)} %get-tuple-element.16.refs_1_, f32[7,4,512]{2,1,0:T(4,128)} %get-tuple-element.17.refs_2_, ...), custom_call_target="tpu_custom_call" | custom-call | tf_op jit(solution)/shard_map/pallas_call | solution.py:811

commit v3 on v2

--- a/solution.py
+++ b/solution.py
@@ -71,6 +71,7 @@
         self.cfg, self.w, self.refs, self.rows = cfg, w, refs, rows
         self.send, self.recv = sems
         self.base = base
+        self.swapped = None
         self.lanes = []
 
     def copy(self, src, dst, index, device):
@@ -120,7 +121,8 @@
 
     def finish(self):
         w, (ny, nz, nx) = self.w, self.cfg
-        self.swapped.wait()
+        if self.swapped is not None:
+            self.swapped.wait()
         per = L // (ny * nz * nx)
         mine, other = self.refs.fin[...], self.refs.swap[...]
         left = jnp.where(w.core == 0, mine, other)
@@ -156,7 +158,7 @@
     def step(self):
         if self.stage > 0:
             self.collect()
-        if self.stage < 3:
+        if self.stage < len(self.order):
             self.launch()
         self.stage += 1
 
@@ -206,10 +208,10 @@
 
 Y, Z, X = 0, 1, 2
 GROUPS = (
+    (6, ((0, 3, 0, HALF, (Y, Z, X)),)),
+    (6, ((0, 3, 0, HALF, (Y, X, Z)),)),
     (6, ((0, 1, 0, HALF, (Y, Z, X)), (1, 1, 0, HALF, (Z, X, Y)), (2, 1, 0, HALF, (X, Y, Z)))),
-    (6, ((0, 3, 0, HALF, (Y, Z, X)),)),
-    (6, ((0, 1, 0, HALF, (Y, Z, X)), (1, 1, 0, HALF, (Z, X, Y)), (2, 1, 0, HALF, (X, Y, Z)))),
-    (2, ((0, 1, 0, 128, (Y, Z, X)), (0, 1, 128, 128, (Z, X, Y)))),
+    (2, ((0, 1, 0, HALF, (Y,)),)),
 )
 
 
@@ -287,7 +289,9 @@
                 v.lanes.append(vm(cfg[axis] - 1, *free, some * 2 * per, width))
                 sems += cfg[axis] - 1
     dma = pltpu.SemaphoreType.DMA
+    v.direct = vm(n - 1, 2 * per, HALF)
     v.w_sem = dma((2,))
+    v.direct_ss, v.direct_rs = dma((n,)), dma((n,))
     v.ids_ss, v.ids_rs = dma((n,)), dma((n,))
     v.fwd_ss, v.fwd_rs = dma((n,)), dma((n,))
     v.back_ss, v.back_rs = dma((n,)), dma((n,))
@@ -410,13 +414,6 @@
     fwd_args = (s.sendbuf, s.recvbuf, cap * B, s.fwd_ss, s.fwd_rs, 1)
     back_args = (s.sendbuf, s.backbuf, cap * B, s.back_ss, s.back_rs, -1)
 
-    def send_all(args):
-        def body(p, _):
-            row_copy(*args, p).start()
-            return 0
-
-        lax.fori_loop(0, n - 1, body, 0)
-
     def sent_all(args):
         def body(p, _):
             row_copy(*args, p).wait_send()
@@ -445,8 +442,6 @@
     s.grid_r[...] = wide(grid_r)
 
     pl.semaphore_wait(barrier, n - 1 + ny - 1)
-    send_all(ids_args)
-
     col = iota((T, T), 1)
     diag = (col & (B - 1)) == (iota((T, T), 0) & (B - 1))
     col_block = (col >> 5).astype(F32)
@@ -464,6 +459,7 @@
 
             @pl.when(p < n - 1)
             def _():
+                row_copy(*ids_args, p).start()
                 row_copy(*fwd_args, p).start()
 
         return 0
@@ -473,6 +469,7 @@
     keep_own(fwd_args)
 
     s.recv_proj[...] = mm(mesh_in[...], encw[2]).astype(BF)
+    out_gin[...] = mm(mesh_in[...], encw[4])
 
     def place(columns):
         col = iota((B, columns), 1)
@@ -490,24 +487,15 @@
     for k in range(4):
         s.H[pl.ds(k * B, B)] = jnp.where(diag_l & (block_l == hidx[k]), 1.0, 0.0).astype(BF)
 
-    def ids_wait(p, _):
-        row_copy(*ids_args, p).wait_recv()
-        return 0
-
-    lax.fori_loop(0, n - 1, ids_wait, 0)
     id_rows = ppt * cap * 8
     id_pick = iota((T, id_rows), 1) == ((iota((T, id_rows), 0) >> 5) << 3)
     id_pick = jnp.where(id_pick, 1.0, 0.0).astype(BF)
 
-    def pick_mesh(t, _):
+    def pick_mesh(t):
         value = mm(id_pick, s.ids_recv[pl.ds(pl.multiple_of(t * id_rows, id_rows), id_rows)])
         value = jnp.concatenate([value, value], axis=1)
-        s.Pm[pl.ds(pl.multiple_of(t * T, T), T)] = jnp.where(
-            diag & (value == col_block), 1.0, 0.0
-        ).astype(BF)
-        return 0
-
-    lax.fori_loop(0, tiles, pick_mesh, 0)
+        return jnp.where(diag & (value == col_block), 1.0, 0.0).astype(BF)
+
     s.acc[...] = jnp.zeros((T, L), F32)
 
     def edge_tile(t, _):
@@ -516,10 +504,12 @@
 
             @pl.when(p < n - 1)
             def _():
+                row_copy(*ids_args, p).wait_recv()
                 row_copy(*fwd_args, p).wait_recv()
 
         at = pl.ds(pl.multiple_of(t * T, T), T)
-        pick = s.Pm[at]
+        pick = pick_mesh(t)
+        s.Pm[at] = pick
         pre = mm(s.recvbuf[at], encw[1]) + mm(pick, s.recv_proj[...])
         s.g_pre[at] = pre.astype(BF)
         act = swish(pre).astype(BF)
@@ -533,10 +523,10 @@
 
     lax.fori_loop(0, tiles, edge_tile, 0)
 
-    def update(u, h, total, wh, wa, wo):
+    def update(u, h, early, total, wa, wo):
         sb = total.astype(BF)
         s.u_s[u][...] = sb
-        gate = mm(h, wh) + mm(sb, wa)
+        gate = early + mm(sb, wa)
         s.u_gate[u][...] = gate.astype(BF)
         hid = swish(gate).astype(BF)
         s.u_hid[u][...] = hid
@@ -569,7 +559,7 @@
             device_id_type=MESH,
         )
 
-    s.lat[0][...] = update(0, mesh_in[...], s.acc[...], encw[4], encw[5], encw[6])
+    s.lat[0][...] = update(0, mesh_in[...], out_gin[...], s.acc[...], encw[5], encw[6])
     proc_copy.wait()
     procw = s.procw
     top, bottom = pl.ds(0, T), pl.ds(T, T)
@@ -587,6 +577,7 @@
         proj[top] = mm(latent, procw[r, 0]).astype(BF)
         proj[bottom] = mm(latent, procw[r, 1]).astype(BF)
         mixed[...] = mm(s.Pc[...], proj[...]).astype(BF)
+        out_gin[...] = mm(latent, procw[r, 3])
         for c in copies:
             c.wait()
         shown = mm(s.halo[r][...], procw[r, 0]).astype(BF)
@@ -599,7 +590,7 @@
         msg = msg.astype(BF)
         s.e_msg[r][...] = msg
         total = tm(s.Pc[:, bottom], msg)
-        new = update(r + 1, latent, total, procw[r, 3], procw[r, 4], procw[r, 5])
+        new = update(r + 1, latent, out_gin[...], total, procw[r, 4], procw[r, 5])
         if r + 1 < ROUNDS:
             s.lat[r + 1][...] = new
         else:
@@ -616,10 +607,10 @@
         sem += 2
         for first, some, left, width, order in lanes:
             rows = (first * 2 * per, some * 2 * per)
-            recvs = s.lanes[lane_at : lane_at + 3]
+            recvs = s.lanes[lane_at : lane_at + len(order)]
             group.lanes.append(Lane(group, recvs, sem, rows, (left, width), order))
-            lane_at += 3
-            sem += ny + nz + nx - 3
+            lane_at += len(order)
+            sem += sum(cfg[axis] - 1 for axis in order)
         groups.append(group)
 
     def outer_pair(p, pair, first, second):
@@ -688,7 +679,6 @@
     groups[1].step()
     lax.fori_loop(tiles // 2, tiles, edge_back, 0)
     keep_own(back_args)
-    groups[0].step()
     drecv = s.acc[...].astype(BF)
     s.drecv[...] = drecv
     out_gin[...] += mt(drecv, encw[2])
@@ -696,7 +686,6 @@
     outer_pair(2, 1, (mesh_in, s.drecv), (mesh_in, s.dgate))
     outer_pair(2, 2, (s.u_s[0], s.dgate), (s.u_hid[0], s.dz))
     groups[2].start_core()
-    groups[0].step()
 
     s.acc[...] = jnp.zeros((T, L), F32)
 
@@ -712,10 +701,9 @@
         s.acc[...] += tm(s.G[at], s.backbuf[at])
         return 0
 
-    lax.fori_loop(0, tiles // 2, back_tile, 0)
+    lax.fori_loop(0, tiles, back_tile, 0)
+    groups[0].step()
     groups[2].add_core()
-    groups[1].step()
-    lax.fori_loop(tiles // 2, tiles, back_tile, 0)
     groups[2].step()
     dgz = norm_back(s.acc[...], s.grid_norm[...].astype(F32), s.grid_r[:, :1]).astype(BF)
     dgpre = (mt(dgz, encw[0]) * swish_grad(s.emb_pre[...].astype(F32))).astype(BF)
@@ -724,17 +712,49 @@
     second = jnp.concatenate([second, jnp.zeros_like(second)], axis=4)
     s.own[3][...] = jnp.concatenate([first, second], axis=3).astype(BF)
     groups[3].start_core()
-    groups[0].start_swap()
-    groups[1].step()
+
+    def direct_copy(p):
+        to = at_offset(p, 1)
+        mine = groups[3].half(w.core)
+        return pltpu.make_async_remote_copy(
+            src_ref=s.own[3].at[w.lat, to // (2 * nx), lax.rem(to // 2, nx), :, mine],
+            dst_ref=s.direct.at[p],
+            send_sem=s.direct_ss.at[p],
+            recv_sem=s.direct_rs.at[p],
+            device_id=(w.lat, to),
+            device_id_type=MESH,
+        )
+
+    def direct_start(p, _):
+        direct_copy(p).start()
+        return 0
+
+    def direct_wait(p, _):
+        direct_copy(p).wait()
+        return 0
+
     groups[3].add_core()
     groups[3].step()
+    groups[1].step()
+    groups[0].step()
+    groups[2].step()
+    groups[3].step()
+    lax.fori_loop(0, n - 1, direct_start, 0)
+    groups[1].step()
+    groups[0].start_swap()
     groups[2].step()
     groups[1].start_swap()
-    groups[3].step()
-    groups[2].step()
-    groups[3].step()
     groups[2].start_swap()
-    groups[3].start_swap()
+    lax.fori_loop(0, n - 1, direct_wait, 0)
+    same = s.own[3][w.lat, w.z, w.x, :, groups[3].half(w.core)].astype(F32)
+    other = jnp.zeros((2 * per, HALF), F32)
+    for p in range(n - 1):
+        if STRIDE * (p + 1) % n % 2 == 0:
+            same = same + s.direct[p].astype(F32)
+        else:
+            other = other + s.direct[p].astype(F32)
+    s.fin[3][...] = same
+    s.swap[3][...] = other
     sent_all(back_args)
 
     left, right = pl.ds(0, HALF), pl.ds(HALF, HALF)

time: 133 us -> 128 us (0.962)
  Pallas kernels: 132 us -> 128 us
    pallas_call x1, Pallas kernels: 130 us -> 126 us  [on_device(): pl.pallas_call(functools.partial(kernel, cfg, n, cap, plan), out_shape=sh...]
where the time goes in v3:
time: 128 us
  Pallas kernels  128 us (100%)
    pallas_call x1, Pallas kernels, on_device(): pl.pallas_call(functools.partial(kernel, cfg, n, cap, plan), out_shape=sh...  126 us

profile of v3, /device:TPU:1, one launch (start us, length us, event | category | flops | bytes accessed | tf_op | source)
XLA Modules:
  0.0 128.3 jit_solution(14995028503208709815)
XLA Ops:
  0.6 125.6 %shard_map.146 = (bf16[256,512]{1,0:T(8,128)(2,1)}, f32[256,512]{1,0:T(8,128)}, f32[7,4,512]{2,1,0:T(4,128)}, f32[2,6,4,512]{3,2,1,0:T(4,128)}, f32[4,227]{1,0:T(4,128)}) custom-call(bf16[227,256]{1,0:T(8,128)(2,1)} %bitcast.5, bf16[256,512]{1,0:T(8,128)(2,1)} %mesh_in.1, bf16[256,512]{1,0:T(8,128)(2,1)} %mgrad.1, bf16[227,512]{1,0:T(8,128)(2,1)} %emb.1, ...), custom_call_target="tpu_custom_call" | custom-call | tf_op jit(solution)/shard_map/pallas_call | solution.py:809
  126.2 2.1 %shard_map.147 = (bf16[256,512]{1,0:T(8,128)(2,1)}, f32[256,512]{1,0:T(8,128)}, f32[7,4,512]{2,1,0:T(4,128)}, f32[2,6,4,512]{3,2,1,0:T(4,128)}, f32[4,227]{1,0:T(4,128)}) custom-call(bf16[256,512]{1,0:T(8,128)(2,1)} %get-tuple-element.15.refs_0_, f32[256,512]{1,0:T(8,128)} %get-tuple-element.16.refs_1_, f32[7,4,512]{2,1,0:T(4,128)} %get-tuple-element.17.refs_2_, ...), custom_call_target="tpu_custom_call" | custom-call | tf_op jit(solution)/shard_map/pallas_call | solution.py:831

commit v4 on v3

--- a/solution.py
+++ b/solution.py
@@ -18,7 +18,7 @@
 MESH = pl.DeviceIdType.MESH
 HALF = L // 2
 OPPOSITE = (1, 0, 3, 2)
-STRIDE = 19
+STRIDE = 13
 
 
 def mm(a, b):

time: 128 us -> 125 us (0.977)
  Pallas kernels: 128 us -> 124 us
    pallas_call x1, Pallas kernels: 126 us -> 122 us  [on_device(): pl.pallas_call(functools.partial(kernel, cfg, n, cap, plan), out_shape=sh...]
where the time goes in v4:
time: 125 us
  Pallas kernels  124 us (99%)
    pallas_call x1, Pallas kernels, on_device(): pl.pallas_call(functools.partial(kernel, cfg, n, cap, plan), out_shape=sh...  122 us

profile of v4, /device:TPU:1, one launch (start us, length us, event | category | flops | bytes accessed | tf_op | source)
XLA Modules:
  0.0 124.8 jit_solution(11220022037376524931)
XLA Ops:
  0.6 122.0 %shard_map.146 = (bf16[256,512]{1,0:T(8,128)(2,1)}, f32[256,512]{1,0:T(8,128)}, f32[7,4,512]{2,1,0:T(4,128)}, f32[2,6,4,512]{3,2,1,0:T(4,128)}, f32[4,227]{1,0:T(4,128)}) custom-call(bf16[227,256]{1,0:T(8,128)(2,1)} %bitcast.5, bf16[256,512]{1,0:T(8,128)(2,1)} %mesh_in.1, bf16[256,512]{1,0:T(8,128)(2,1)} %mgrad.1, bf16[227,512]{1,0:T(8,128)(2,1)} %emb.1, ...), custom_call_target="tpu_custom_call" | custom-call | tf_op jit(solution)/shard_map/pallas_call | solution.py:809
  122.7 2.1 %shard_map.147 = (bf16[256,512]{1,0:T(8,128)(2,1)}, f32[256,512]{1,0:T(8,128)}, f32[7,4,512]{2,1,0:T(4,128)}, f32[2,6,4,512]{3,2,1,0:T(4,128)}, f32[4,227]{1,0:T(4,128)}) custom-call(bf16[256,512]{1,0:T(8,128)(2,1)} %get-tuple-element.15.refs_0_, f32[256,512]{1,0:T(8,128)} %get-tuple-element.16.refs_1_, f32[7,4,512]{2,1,0:T(4,128)} %get-tuple-element.17.refs_2_, ...), custom_call_target="tpu_custom_call" | custom-call | tf_op jit(solution)/shard_map/pallas_call | solution.py:831
